TPU v7x, 512 devices: a whole 4x4x16 slice. The times are simulated.
512 devices in a mesh: seq: 64 (over y, z), head: 8 (over x, core).
Axes of the slice: x: 4, y: 4, z: 16, core: 2. Of those that a mesh axis runs over, the one named last changes fastest.
Arguments:
- query: bfloat16 [16384, 2048], P('seq', 'head'), may hold values from -6 to 6
- key: bfloat16 [16384, 2048], P('seq', 'head'), may hold values from -6 to 6
- value: bfloat16 [16384, 2048], P('seq', 'head'), may hold values from -6 to 6
- output: bfloat16 [16384, 2048], P('seq', 'head'), may hold values from -6 to 6
- grad_out: bfloat16 [16384, 2048], P('seq', 'head'), may hold values from -6 to 6
- logsumexp: float32 [16, 16384], P('head', 'seq'), as said below
- remote_blocks: int32 [128, 8], P('seq'), may hold values from 0 to 127, as said below
- remote_count: int32 [128], P('seq'), may hold values from 1 to 8
Outputs:
- grad_query: bfloat16 [16384, 2048], P('seq', 'head')
- grad_key: bfloat16 [16384, 2048], P('seq', 'head')
- grad_value: bfloat16 [16384, 2048], P('seq', 'head')
Inputs may be any that keep to these rules, and one draw needn't show every extreme that they name: Entries remote_blocks[q, r] with r >= remote_count[q] are not used. The used entries of query block q lie in runs of 2 blocks (index // 2) other than q's own run, none within 1 of q, and among all query blocks of one run no two used entries lie in the same run. `logsumexp`: each entry lies within 1 of log((3 + 9 / 2) * 128) + 0.5.
All inputs are finite; a program needn't handle non-finite values.
Results may differ from a plain program's by a relative error of at most 0.0054.
Values may be sent and summed in bfloat16 or wider, within the bound.
A program may use at most 128 MiB of HBM per device.

v0:
```python
import jax
import jax.numpy as jnp
from jax import lax
from jax.sharding import PartitionSpec as P

HD = 128
BLOCK = 128


def with_halo(cells, sides, width):
    for axis, dim in sides:
        count = lax.axis_size(axis)
        ends = count - 1
        head = lax.slice_in_dim(cells, 0, width, axis=dim)
        tail = lax.slice_in_dim(cells, cells.shape[dim] - width, cells.shape[dim], axis=dim)
        cells = jnp.concatenate(
            [
                lax.ppermute(tail, axis, [(i, (i + 1) % count) for i in range(ends)]),
                cells,
                lax.ppermute(head, axis, [((i + 1) % count, i) for i in range(ends)]),
            ],
            axis=dim,
        )
    return cells


def block_pairs(queries, grads, stats, keys, values, valid, scale):
    scores = (
        jnp.einsum("pxhd,pyhd->phxy", queries, keys, preferred_element_type=jnp.float32) * scale
    )
    weights = jnp.exp(scores - stats[0][..., None]) * valid[:, None, None, None]
    probs = weights.astype(jnp.bfloat16)
    grad_values = jnp.einsum("phxy,pxhd->pyhd", probs, grads, preferred_element_type=jnp.float32)
    grad_probs = jnp.einsum("pxhd,pyhd->phxy", grads, values, preferred_element_type=jnp.float32)
    grad_scores = (weights * (grad_probs - stats[1][..., None])).astype(jnp.bfloat16)
    grad_queries = (
        jnp.einsum("phxy,pyhd->pxhd", grad_scores, keys, preferred_element_type=jnp.float32) * scale
    )
    grad_keys = (
        jnp.einsum("phxy,pxhd->pyhd", grad_scores, queries, preferred_element_type=jnp.float32)
        * scale
    )
    return (grad_queries, grad_keys, grad_values)


def spread_terms(terms):
    padded = jnp.pad(terms[0], ((0, 2), (0, 0), (0, 0), (0, 0)))
    padded = padded + jnp.pad(terms[1], ((1, 1), (0, 0), (0, 0), (0, 0)))
    return padded + jnp.pad(terms[2], ((2, 0), (0, 0), (0, 0), (0, 0)))


def remote_pairs(
    part_query, part_grad, part_stats, key_table, value_table, key_index, live_in, scale
):
    senders = part_query.shape[0]
    head_count = part_query.shape[2]
    groups = senders // 8

    def remote_group(items):
        one_q, one_g, one_s, one_k, one_l = items
        return block_pairs(
            one_q,
            one_g,
            one_s.transpose(1, 0, 2, 3),
            key_table[one_k],
            value_table[one_k],
            one_l,
            scale,
        )

    group_shape = (groups, 8, BLOCK, head_count, HD)
    found_q, found_k, found_v = lax.map(
        remote_group,
        (
            part_query.reshape(group_shape),
            part_grad.reshape(group_shape),
            part_stats.reshape(groups, 8, 2, head_count, BLOCK),
            key_index.reshape(groups, 8),
            live_in.reshape(groups, 8),
        ),
    )
    out_shape = (senders, BLOCK, head_count, HD)
    return (found_q.reshape(out_shape), found_k.reshape(out_shape), found_v.reshape(out_shape))


def per_device(query, key, value, output, grad_out, logsumexp, remote_blocks, remote_count):
    seq_size = lax.axis_size("seq")
    place = lax.axis_index("seq")
    rows, width = query.shape
    count_blocks = rows // BLOCK
    heads_here = width // HD
    scale = float(HD) ** (-0.5)
    shape_four = (count_blocks, BLOCK, heads_here, HD)
    q_tiles = query.reshape(shape_four)
    g_tiles = grad_out.reshape(shape_four)
    k_tiles = key.reshape(shape_four)
    v_tiles = value.reshape(shape_four)
    delta = jnp.sum(
        grad_out.astype(jnp.float32).reshape(shape_four)
        * output.astype(jnp.float32).reshape(shape_four),
        axis=3,
    )
    stats = jnp.stack(
        [
            logsumexp.reshape(heads_here, count_blocks, BLOCK).transpose(1, 0, 2),
            delta.transpose(0, 2, 1),
        ]
    )
    slots_used = (
        jnp.arange(remote_blocks.shape[1], dtype=jnp.int32)[None, :] < remote_count[:, None]
    )
    owners = remote_blocks // count_blocks
    local_key = remote_blocks % count_blocks
    match = (
        (owners[:, :, None] == jnp.arange(seq_size, dtype=jnp.int32)[None, None, :])
        & slots_used[:, :, None]
    ).astype(jnp.int32)
    live = jnp.sum(match, axis=(0, 1))
    send_query = jnp.sum(
        match * jnp.arange(count_blocks, dtype=jnp.int32)[:, None, None], axis=(0, 1)
    )
    send_key = jnp.sum(match * local_key[:, :, None], axis=(0, 1))
    meta = jnp.stack([send_key, live], axis=1).astype(jnp.float32)
    got_stats, got_meta = (
        lax.all_to_all(
            stats[:, send_query].transpose(1, 0, 2, 3),
            "seq",
            split_axis=0,
            concat_axis=0,
            tiled=True,
        ),
        lax.all_to_all(meta, "seq", split_axis=0, concat_axis=0, tiled=True),
    )
    key_index = got_meta[:, 0].astype(jnp.int32)
    live_in = got_meta[:, 1]
    got_query, got_grad = (
        lax.all_to_all(q_tiles[send_query], "seq", split_axis=0, concat_axis=0, tiled=True),
        lax.all_to_all(g_tiles[send_query], "seq", split_axis=0, concat_axis=0, tiled=True),
    )
    remote_q, remote_k, remote_v = remote_pairs(
        got_query, got_grad, got_stats, k_tiles, v_tiles, key_index, live_in, scale
    )
    returned = lax.all_to_all(
        remote_q.astype(jnp.bfloat16), "seq", split_axis=0, concat_axis=0, tiled=True
    )
    empty = jnp.zeros((count_blocks, BLOCK, width), jnp.float32)
    grad_key = empty.at[key_index].add(remote_k.reshape(seq_size, BLOCK, width))
    grad_value = empty.at[key_index].add(remote_v.reshape(seq_size, BLOCK, width))
    grad_query = empty.at[send_query].add(
        returned.reshape(seq_size, BLOCK, width).astype(jnp.float32)
    )
    offsets = jnp.arange(3, dtype=jnp.int32)[:, None]
    band_index = (
        place * count_blocks + jnp.arange(count_blocks, dtype=jnp.int32)[None, :] + offsets - 1
    )
    band_ok = (
        ((band_index >= 0) & (band_index < count_blocks * seq_size)).astype(jnp.float32).reshape(-1)
    )
    rimmed = with_halo(jnp.stack([key, value]), (("seq", 1),), BLOCK)
    wide = rimmed.reshape(2, count_blocks + 2, BLOCK, heads_here, HD)
    band_keys = jnp.concatenate([wide[0, j : j + count_blocks] for j in range(3)])
    band_values = jnp.concatenate([wide[1, j : j + count_blocks] for j in range(3)])
    band_q, band_k, band_v = block_pairs(
        jnp.concatenate([q_tiles] * 3),
        jnp.concatenate([g_tiles] * 3),
        jnp.concatenate([stats] * 3, axis=1),
        band_keys,
        band_values,
        band_ok,
        scale,
    )
    grad_query = grad_query + jnp.sum(band_q.reshape(3, count_blocks, BLOCK, width), axis=0)
    spread_k = spread_terms(band_k.reshape(3, count_blocks, BLOCK, heads_here, HD))
    spread_v = spread_terms(band_v.reshape(3, count_blocks, BLOCK, heads_here, HD))
    both = jnp.stack([spread_k, spread_v]).reshape(2, count_blocks + 2, BLOCK, width)
    edges = jnp.stack([both[:, 0], both[:, count_blocks + 1]])
    arrived = with_halo(edges, (("seq", 0),), 1)
    own = both[:, 1 : count_blocks + 1]
    own = own.at[:, 0].add(arrived[0]).at[:, count_blocks - 1].add(arrived[3])
    grad_key = grad_key + own[0]
    grad_value = grad_value + own[1]
    return (
        grad_query.reshape(rows, width).astype(jnp.bfloat16),
        grad_key.reshape(rows, width).astype(jnp.bfloat16),
        grad_value.reshape(rows, width).astype(jnp.bfloat16),
    )


def solution(mesh):
    return jax.shard_map(
        per_device,
        mesh=mesh,
        in_specs=(
            P("seq", "head"),
            P("seq", "head"),
            P("seq", "head"),
            P("seq", "head"),
            P("seq", "head"),
            P("head", "seq"),
            P("seq", None),
            P("seq"),
        ),
        out_specs=(P("seq", "head"), P("seq", "head"), P("seq", "head")),
        check_vma=False,
    )
```

profile of v0, /device:TPU:24, one launch (start us, length us, event | category | flops | bytes accessed | tf_op | source)
XLA Modules:
  0.0 823.8 jit_solution(14635319618601876058)
XLA Ops:
  2.9 18.7 %all-to-all-start = ((f32[64,1,2]{2,1,0:T(1,128)}), f32[64,1,2]{2,1,0:T(1,128)S(1)}, u32[]{:S(2)}, u32[]{:S(2)}) async-start(f32[64,1,2]{2,1,0:T(1,128)} %copy.175), calls=%async_computation | async-start | bytes 65536 | tf_op jit(solution)/shard_map/all_to_all | solution.py:132
  23.9 1.4 gather_fusion.3
  25.3 8.8 %all-to-all-done = f32[64,1,2]{2,1,0:T(1,128)S(1)} async-done(((f32[64,1,2]{2,1,0:T(1,128)}), f32[64,1,2]{2,1,0:T(1,128)S(1)}, u32[]{:S(2)}, u32[]{:S(2)}) %all-to-all-start) | async-done | bytes 544 | tf_op jit(solution)/shard_map/all_to_all | solution.py:132
  34.1 6.5 all-to-all-start.2
  41.5 10.5 %gather_fusion.2 = bf16[64,128,2,128]{3,2,1,0:T(2,128)(2,1)} fusion(bf16[2,128,2,128]{3,2,1,0:T(2,128)(2,1)S(1)} %reshape.279, s32[1024]{0:T(1024)S(1)} %pad_clamp_fusion.1), kind=kCustom, calls=%fused_computation.2 | custom fusion | bytes 8388864 | tf_op jit(solution)/shard_map/gather | solution.py:137
  52.0 3.2 all-to-all-done.2
  55.3 12.1 %all-to-all-start.1 = ((bf16[64,128,2,128]{3,2,1,0:T(2,128)(2,1)}), bf16[64,128,2,128]{3,2,1,0:T(2,128)(2,1)}, u32[]{:S(2)}, u32[]{:S(2)}) async-start(bf16[64,128,2,128]{3,2,1,0:T(2,128)(2,1)} %gather_fusion.2), calls=%async_computation.1 | async-start | bytes 8388608 | tf_op jit(solution)/shard_map/all_to_all | solution.py:137
  67.4 10.5 %gather_fusion.4 = bf16[64,128,2,128]{3,2,1,0:T(2,128)(2,1)} fusion(bf16[2,128,2,128]{3,2,1,0:T(2,128)(2,1)S(1)} %reshape.281, s32[1024]{0:T(1024)S(1)} %pad_clamp_fusion.1), kind=kCustom, calls=%fused_computation.4 | custom fusion | bytes 8388864 | tf_op jit(solution)/shard_map/gather | solution.py:138
  78.0 173.7 %all-to-all-done.1 = bf16[64,128,2,128]{3,2,1,0:T(2,128)(2,1)} async-done(((bf16[64,128,2,128]{3,2,1,0:T(2,128)(2,1)}), bf16[64,128,2,128]{3,2,1,0:T(2,128)(2,1)}, u32[]{:S(2)}, u32[]{:S(2)}) %all-to-all-start.1) | async-done | bytes 4194336 | tf_op jit(solution)/shard_map/all_to_all | solution.py:137
  251.7 10.0 %all-to-all-start.3 = ((bf16[64,128,2,128]{3,2,1,0:T(2,128)(2,1)}), bf16[64,128,2,128]{3,2,1,0:T(2,128)(2,1)}, u32[]{:S(2)}, u32[]{:S(2)}) async-start(bf16[64,128,2,128]{3,2,1,0:T(2,128)(2,1)} %gather_fusion.4), calls=%async_computation.3 | async-start | bytes 8388608 | tf_op jit(solution)/shard_map/all_to_all | solution.py:138
  262.1 185.3 %all-to-all-done.3 = bf16[64,128,2,128]{3,2,1,0:T(2,128)(2,1)} async-done(((bf16[64,128,2,128]{3,2,1,0:T(2,128)(2,1)}), bf16[64,128,2,128]{3,2,1,0:T(2,128)(2,1)}, u32[]{:S(2)}, u32[]{:S(2)}) %all-to-all-start.3) | async-done | bytes 4194336 | tf_op jit(solution)/shard_map/all_to_all | solution.py:138
  447.4 86.3 %while.16 = (s32[]{:T(128)}, bf16[8,8,128,2,128]{2,4,3,1,0:T(8,128)(2,1)}, f32[8,8,128,2,128]{2,4,3,1,0:T(8,128)}, f32[8,8,128,2,128]{2,4,3,1,0:T(8,128)}, s32[8...) while((s32[]{:T(128)}, ...), condition=%wide.region_6.7_spmd, body=%wide.region_5.6_spmd.sunk | while | flops 337904672 | bytes 16863640 | solution.py:72
  447.4 1.6 gather_fusion.1
  449.1 1.6 gather_fusion
  451.1 2.0 constant_dynamic-slice_fusion.9
  455.5 1.4 fusion.89
  458.3 1.6 gather_fusion.1
  459.9 1.6 gather_fusion
  461.9 2.0 constant_dynamic-slice_fusion.9
  467.6 1.4 fusion.88
  469.0 1.6 gather_fusion.1
  470.7 1.6 gather_fusion
  472.7 2.0 constant_dynamic-slice_fusion.9
  478.4 1.4 fusion.88
  479.8 1.6 gather_fusion.1
  481.4 1.6 gather_fusion
  483.5 2.0 constant_dynamic-slice_fusion.9
  487.8 1.4 fusion.89
  489.1 1.3 fusion.88
  490.5 1.6 gather_fusion.1
  492.2 1.6 gather_fusion
  494.2 2.0 constant_dynamic-slice_fusion.9
  498.6 1.4 fusion.89
  500.0 1.3 fusion.88
  501.4 1.6 gather_fusion.1
  503.0 1.6 gather_fusion
  505.0 2.0 constant_dynamic-slice_fusion.9
  509.4 1.3 fusion.89
  510.7 1.4 fusion.88
  512.1 1.6 gather_fusion.1
  513.8 1.6 gather_fusion
  515.8 2.0 constant_dynamic-slice_fusion.9
  520.2 1.3 fusion.89
  521.5 1.4 fusion.88
  522.9 1.6 gather_fusion.1
  524.5 1.6 gather_fusion
  526.6 2.0 constant_dynamic-slice_fusion.9
  530.9 1.3 fusion.89
  532.3 1.4 fusion.88
  533.6 10.1 %all-to-all-start.4 = ((bf16[64,128,2,128]{1,3,2,0:T(8,128)(2,1)}), bf16[64,128,2,128]{1,3,2,0:T(8,128)(2,1)}, u32[]{:S(2)}, u32[]{:S(2)}) async-start(bf16[64,128,2,128]{1,3,2,0:T(8,128)(2,1)} %bitcast.162), calls=%async_computation.4 | async-start | bytes 8388608 | tf_op jit(solution)/shard_map/all_to_all | solution.py:143
  543.8 3.4 collective-permute-start
  547.2 4.6 collective-permute-start.1
  552.1 176.7 %collective-permute-done = bf16[2,128,256]{2,1,0:T(8,128)(2,1)S(1)} collective-permute-done((bf16[2,128,256]{2,1,0:T(8,128)(2,1)S(1)}, bf16[2,128,256]{2,1,0:T(8,128)(2,1)S(1)}, u32[]{:S(2)}, u32[]{:S(2)}) %collective-permute-start) | collective-permute-done | bytes 131104 | tf_op jit(solution)/shard_map/ppermute | solution.py:18
  731.9 1.9 collective-permute-start.2
  733.9 9.2 %collective-permute-done.2 = f32[1,2,128,256]{3,2,1,0:T(8,128)S(1)} collective-permute-done((f32[1,2,128,256]{3,2,1,0:T(8,128)S(1)}, f32[1,2,128,256]{3,2,1,0:T(8,128)S(1)}, u32[]{:S(2)}, u32[]{:S(2)}) %collective-permute-start.2) | collective-permute-done | bytes 262176 | tf_op jit(solution)/shard_map/ppermute | solution.py:18
  743.1 2.1 collective-permute-start.3
  745.9 5.5 collective-permute-done.3
  751.5 9.0 %copy.190 = f32[64,128,256]{2,1,0:T(8,128)} copy(f32[64,128,256]{1,2,0:T(8,128)} %bitcast.160) | data formatting | bytes 16777216 | tf_op jit(solution)/shard_map/reshape;reshape | solution.py:148
  760.5 12.3 %scatter_fusion.2 = f32[2,128,256]{2,1,0:T(8,128)S(1)} fusion(f32[2,128,256]{2,1,0:T(8,128)S(1)} %get-tuple-element.179, s32[64]{0:T(128)S(1)} %get-tuple-element.191, f32[64,128,256]{2,1,0:T(8,128)} %copy.190), kind=kCustom, calls=%fused_computation.7 | custom fusion | flops 2097152 | bytes 25166080 | tf_op jit(solution)/shard_map/scatter-add | solution.py:148
  773.4 9.0 %copy.189 = f32[64,128,256]{2,1,0:T(8,128)} copy(f32[64,128,256]{1,2,0:T(8,128)} %bitcast.161) | data formatting | bytes 16777216 | tf_op jit(solution)/shard_map/reshape;reshape | solution.py:147
  782.4 12.3 %scatter_fusion.1 = f32[2,128,256]{2,1,0:T(8,128)S(1)} fusion(f32[2,128,256]{2,1,0:T(8,128)S(1)} %get-tuple-element.180, s32[64]{0:T(128)S(1)} %get-tuple-element.191, f32[64,128,256]{2,1,0:T(8,128)} %copy.189), kind=kCustom, calls=%fused_computation.6 | custom fusion | flops 2097152 | bytes 25166080 | tf_op jit(solution)/shard_map/scatter-add | solution.py:147
  795.4 6.5 bitcast_convert_fusion
  801.9 9.0 %copy.198 = f32[64,128,256]{2,1,0:T(8,128)} copy(f32[64,128,256]{1,2,0:T(8,128)} %bitcast_convert_fusion) | data formatting | bytes 16777216 | tf_op jit(solution)/shard_map/convert_element_type | solution.py:150
  810.8 12.3 %scatter_fusion = f32[2,128,256]{2,1,0:T(8,128)S(1)} fusion(f32[2,128,256]{2,1,0:T(8,128)S(1)} %copy.182, s32[64]{0:T(128)S(1)} %fusion.46, f32[64,128,256]{2,1,0:T(8,128)} %copy.198), kind=kCustom, calls=%fused_computation.5 | custom fusion | flops 2097152 | bytes 25166080 | tf_op jit(solution)/shard_map/scatter-add | solution.py:149
  (150 shorter events, 38.6 us)
Async XLA Ops:
  2.9 31.2 %all-to-all-start = ((f32[64,1,2]{2,1,0:T(1,128)}), f32[64,1,2]{2,1,0:T(1,128)S(1)}, u32[]{:S(2)}, u32[]{:S(2)}) async-start(f32[64,1,2]{2,1,0:T(1,128)} %copy.175), calls=%async_computation | async-start | bytes 65536 | tf_op jit(solution)/shard_map/all_to_all | solution.py:132
  34.1 21.2 %all-to-all-start.2 = ((f32[64,2,2,128]{3,2,1,0:T(2,128)}), f32[64,2,2,128]{3,2,1,0:T(2,128)S(1)}, u32[]{:S(2)}, u32[]{:S(2)}) async-start(f32[64,2,2,128]{3,2,1,0:T(2,128)} %gather_fusion.3), calls=%async_computation.2 | async-start | bytes 262144 | tf_op jit(solution)/shard_map/all_to_all | solution.py:125
  41.5 25.9 %copy-start.2 = (bf16[256,256]{1,0:T(8,128)(2,1)S(1)}, bf16[256,256]{1,0:T(8,128)(2,1)}, u32[]{:S(2)}) copy-start(bf16[256,256]{1,0:T(8,128)(2,1)} %param.18) | copy-start | bytes 393220
  55.3 196.4 %all-to-all-start.1 = ((bf16[64,128,2,128]{3,2,1,0:T(2,128)(2,1)}), bf16[64,128,2,128]{3,2,1,0:T(2,128)(2,1)}, u32[]{:S(2)}, u32[]{:S(2)}) async-start(bf16[64,128,2,128]{3,2,1,0:T(2,128)(2,1)} %gather_fusion.2), calls=%async_computation.1 | async-start | bytes 8388608 | tf_op jit(solution)/shard_map/all_to_all | solution.py:137
  67.4 194.3 %copy-start = (bf16[256,256]{1,0:T(8,128)(2,1)S(1)}, bf16[256,256]{1,0:T(8,128)(2,1)}, u32[]{:S(2)}) copy-start(bf16[256,256]{1,0:T(8,128)(2,1)} %param.15) | copy-start | bytes 393220
  67.4 194.4 %copy-start.1 = (bf16[256,256]{1,0:T(8,128)(2,1)S(1)}, bf16[256,256]{1,0:T(8,128)(2,1)}, u32[]{:S(2)}) copy-start(bf16[256,256]{1,0:T(8,128)(2,1)} %param.16) | copy-start | bytes 393220
  251.7 195.7 %all-to-all-start.3 = ((bf16[64,128,2,128]{3,2,1,0:T(2,128)(2,1)}), bf16[64,128,2,128]{3,2,1,0:T(2,128)(2,1)}, u32[]{:S(2)}, u32[]{:S(2)}) async-start(bf16[64,128,2,128]{3,2,1,0:T(2,128)(2,1)} %gather_fusion.4), calls=%async_computation.3 | async-start | bytes 8388608 | tf_op jit(solution)/shard_map/all_to_all | solution.py:138
  533.6 18.2 %copy-start.3 = (f32[2,256]{1,0:T(2,128)S(1)}, f32[2,256]{1,0:T(2,128)}, u32[]{:S(2)}) copy-start(f32[2,256]{1,0:T(2,128)} %param.19) | copy-start | bytes 6148
  533.6 261.7 %all-to-all-start.4 = ((bf16[64,128,2,128]{1,3,2,0:T(8,128)(2,1)}), bf16[64,128,2,128]{1,3,2,0:T(8,128)(2,1)}, u32[]{:S(2)}, u32[]{:S(2)}) async-start(bf16[64,128,2,128]{1,3,2,0:T(8,128)(2,1)} %bitcast.162), calls=%async_computation.4 | async-start | bytes 8388608 | tf_op jit(solution)/shard_map/all_to_all | solution.py:143
  543.8 187.5 %copy-start.4 = (pred[4]{0:T(512)(128)(4,1)S(1)}, pred[4]{0:T(512)(128)(4,1)}, u32[]{:S(2)}) copy-start(pred[4]{0:T(512)(128)(4,1)} %constant.129.clone.1) | copy-start | bytes 16
  543.8 185.0 %collective-permute-start = (bf16[2,128,256]{2,1,0:T(8,128)(2,1)S(1)}, bf16[2,128,256]{2,1,0:T(8,128)(2,1)S(1)}, u32[]{:S(2)}, u32[]{:S(2)}) collective-permute-start(bf16[2,128,256]{2,1,0:T(8,128)(2,1)S(1)} %get-tuple-element.187), channel_id=1, source_target_pairs={{0,8},{8,16},{16,24},{24,32},{32,40},{40,48},{48,56},{56,64},{64,7... | collective-permute-start | bytes 393224 | tf_op jit(solution)/shard_map/ppermute | solution.py:18
  547.2 181.6 %collective-permute-start.1 = (bf16[2,128,256]{2,1,0:T(8,128)(2,1)S(1)}, bf16[2,128,256]{2,1,0:T(8,128)(2,1)S(1)}, u32[]{:S(2)}, u32[]{:S(2)}) collective-permute-start(bf16[2,128,256]{2,1,0:T(8,128)(2,1)S(1)} %get-tuple-element.188), channel_id=1, source_target_pairs={{8,0},{16,8},{24,16},{32,24},{40,32},{48,40},{56,48},{64,56},{72,6... | collective-permute-start | bytes 393224 | tf_op jit(solution)/shard_map/ppermute | solution.py:20
  731.9 11.1 %collective-permute-start.2 = (f32[1,2,128,256]{3,2,1,0:T(8,128)S(1)}, f32[1,2,128,256]{3,2,1,0:T(8,128)S(1)}, u32[]{:S(2)}, u32[]{:S(2)}) collective-permute-start(f32[1,2,128,256]{3,2,1,0:T(8,128)S(1)} %fusion.33), channel_id=1, source_target_pairs={{0,8},{8,16},{16,24},{24,32},{32,40},{40,48},{48,56},{56,64},{64,7... | collective-permute-start | bytes 786440 | tf_op jit(solution)/shard_map/ppermute | solution.py:18
  743.1 8.3 %collective-permute-start.3 = (f32[1,2,128,256]{3,2,1,0:T(8,128)S(1)}, f32[1,2,128,256]{3,2,1,0:T(8,128)S(1)}, u32[]{:S(2)}, u32[]{:S(2)}) collective-permute-start(f32[1,2,128,256]{3,2,1,0:T(8,128)S(1)} %get-tuple-element.173), channel_id=1, source_target_pairs={{8,0},{16,8},{24,16},{32,24},{40,32},{48,40},{56,48},{64,56},{72,6... | collective-permute-start | bytes 786440 | tf_op jit(solution)/shard_map/ppermute | solution.py:20
where the time goes:
time: 826 us; the launch traced here: 824 us
  waiting for transfers between devices  562 us (68%)
  local copies, waits for them, and re-layouts  98.6 us (12%)
  starting transfers between devices  69.4 us (8%)
  other arithmetic  49.5 us (6%)
  matrix products  42.3 us (5%)
    ppermute x2, waiting for transfers between devices, with_halo(): lax.ppermute(tail, axis, [(i, (i + 1) % count) for i in range(ends)])  186 us
    all_to_all x1, waiting for transfers between devices, per_device(): lax.all_to_all(g_tiles[send_query], 'seq', split_axis=0, concat_axis=0, t...  185 us
    all_to_all x1, waiting for transfers between devices, per_device(): lax.all_to_all(q_tiles[send_query], 'seq', split_axis=0, concat_axis=0, t...  174 us
    all_to_all x1, starting transfers between devices, per_device(): lax.all_to_all(meta, 'seq', split_axis=0, concat_axis=0, tiled=True)  18.7 us
  transfers between devices with their start and end apart: 9, of which 7 were waited for; matrix products, arithmetic and copies ran while one was open for 9% of the time, Pallas kernels for 0%

commit v1 on v0

--- a/solution.py
+++ b/solution.py
@@ -1,10 +1,24 @@
+import functools
+
 import jax
 import jax.numpy as jnp
 from jax import lax
+from jax.experimental import pallas as pl
+from jax.experimental.pallas import tpu as pltpu
 from jax.sharding import PartitionSpec as P
 
 HD = 128
 BLOCK = 128
+NY = 4
+SLOTS = 9
+RELAY = 4
+FRONT = SLOTS - RELAY
+OWN = 12
+DEAD = 1e30
+LOG2E = 1.4426950408889634
+F32 = jnp.float32
+BF16 = jnp.bfloat16
+I32 = jnp.int32
 
 
 def with_halo(cells, sides, width):
@@ -83,7 +97,7 @@
     return (found_q.reshape(out_shape), found_k.reshape(out_shape), found_v.reshape(out_shape))
 
 
-def per_device(query, key, value, output, grad_out, logsumexp, remote_blocks, remote_count):
+def general(query, key, value, output, grad_out, logsumexp, remote_blocks, remote_count):
     seq_size = lax.axis_size("seq")
     place = lax.axis_index("seq")
     rows, width = query.shape
@@ -183,6 +197,702 @@
         grad_query.reshape(rows, width).astype(jnp.bfloat16),
         grad_key.reshape(rows, width).astype(jnp.bfloat16),
         grad_value.reshape(rows, width).astype(jnp.bfloat16),
+    )
+
+
+def dot(a, b, ca, cb):
+    return lax.dot_general(a, b, (((ca,), (cb,)), ((), ())), preferred_element_type=F32)
+
+
+FINE = (0, 1)
+CHAINS = [(u, j) for u in range(6) for j in ((0, 1) if u in FINE else (2,))]
+
+
+def last(u, j, d, half):
+    if j < 2:
+        return half if j == d else half - 1
+    return half if u < 4 or d == 0 else half - 1
+
+
+def plan(half, release=(0, 7, 3), lat=2.0, chunk=0.35, tab=4.0, bw=51.2, hop=0.3, iss=0.1):
+    F, R = SLOTS, RELAY
+    mid = half // 2
+    steps = {}
+
+    for u, j in CHAINS:
+        cut = u > 3
+        for d in range(2):
+            for k in range(last(u, j, d, half) + 1):
+                def size(n):
+                    return 4 if u > 3 else 64 if n < half and j == 2 else 32
+                sends = []
+                if k < last(u, j, d, half) and not (cut and k == mid):
+                    sends.append((("z", u, j, d, k + 1), d, size(k + 1), 1))
+                if k == 0 and cut and mid < last(u, j, d, half):
+                    sends.append((("z", u, j, d, mid + 1), d, size(mid + 1), mid + 1))
+                needs = [("z", u, j, d, k - 1)] if k else []
+                if k == 0 and 0 < u < 4:
+                    pj = 0 if u - 1 in FINE else 2
+                    needs = [("z", u - 1, pj, d, min(release[u - 1], half - 1))]
+                awaits = [("z", u, j, d, k)] if k else []
+                steps["z", u, j, d, k] = (needs, awaits, sends, 0.0)
+
+    def all_in(u):
+        return [("z", c, j, d, last(c, j, d, half)) for c, j in CHAINS if c == u for d in range(2)]
+
+    steps["tab",] = (all_in(5), [], [], tab)
+    stats_in = all_in(4)
+    for u in (4, 5):
+        steps["zq", u] = ([("tab",)] + all_in(u), [], [], 0.5)
+    for h in range(2):
+        got = [all_in(2 * h + t) for t in range(2)]
+        pairs = []
+        for i in range(OWN // 4):
+            steps["own", h, i] = ([("tab",)] + stats_in + got[0] + got[1], [], [], 2 * chunk)
+            pairs.append(("own", h, i))
+        for d in range(2):
+            for t in range(3):
+                kib = 32 if t < 2 else 4
+                needs = [("tab",)] + (got[t] if t < 2 else stats_in)
+                if t < 2:
+                    sends = [
+                        (("yb", h, t, d), 2 + d, R * kib, 1),
+                        (("y", h, t, d), 2 + d, (F - R) * kib, 1),
+                    ]
+                else:
+                    sends = [(("yb", h, t, d), 2 + d, F * kib, 1)]
+                steps["pk", h, t, d] = (needs, [], sends, 0.25)
+                steps["f", h, t, d] = ([], [("yb", h, t, d)], [(("f", h, t, d), 2 + d, R * kib, 1)], 0.0)
+            seen = [("f", h, t, d) for t in range(3)]
+            ym = [("y", h, t, d) for t in range(2)]
+            steps["far", h, d] = ([], seen, [(("r2", h, d), 3 - d, R * 32, 1)], R / 2 * chunk)
+            steps["na", h, d] = (seen, ym, [(("r1", h, d, 0), 3 - d, (F - R) * 32, 1)], (F - R) / 2 * chunk)
+            steps["nb", h, d] = (seen, [("r2", h, d)], [(("r1", h, d, 1), 3 - d, R * 32, 1)], R / 2 * chunk)
+            pairs += [("far", h, d), ("na", h, d), ("nb", h, d)]
+        back = [("r1", h, d, part) for d in range(2) for part in range(2)]
+        steps["w", h] = (pairs, back, [], 0.1)
+        steps["kv", h] = (pairs, [], [], 0.2)
+        fin = []
+        for d in range(2):
+            for j in range(2):
+                for k in range(1, half + 1):
+                    if k > 1 or j == d:
+                        first = k == 1 or (k == 2 and j != d) or k == mid + 1
+                        awaits = [] if first else [("s", h, d, j, k - 1)]
+                        hops = mid + 1 if k == mid else 1
+                        if k in (mid, half):
+                            fin.append(("s", h, d, j, k))
+                        steps["s", h, d, j, k] = ([("w", h)], awaits, [(("s", h, d, j, k), 1 - d, 32, hops)], 0.12)
+        for t in range(2):
+            steps["zq", 2 * h + t] = (got[t] + [("pk", h, t, 1)], [], [], 0.5)
+        steps["yq", h] = ([("s", h, 0, 0, half // 2 + 1)], [], [], 0.5)
+        steps["e", h] = ([("w", h)], fin, [], 0.3)
+    for s in list(steps):
+        n, a, sd, c = steps[s]
+        steps[s] = (n, a, sd, c + iss * (len(a) + len(sd)))
+    sender = {m: (s, kib, hops) for s, (_, _, sends, _) in steps.items() for m, _, kib, hops in sends}
+    after = {s: [] for s in steps}
+    for s, (needs, awaits, _, _) in steps.items():
+        for n in needs:
+            after[n].append((s, 0.0))
+        for m in awaits:
+            f, kib, hops = sender[m]
+            after[f].append((s, hops * kib / bw + lat + hop * (hops - 1)))
+    way = {}
+
+    def length(s):
+        if s not in way:
+            way[s] = steps[s][3] + max([gap + length(n) for n, gap in after[s]], default=0.0)
+        return way[s]
+
+    left = sorted(steps, key=lambda s: (-length(s), str(s)))
+    now, free, arrival, done, order = 0.0, [0.0] * 4, {}, set(), []
+    while left:
+        ready = [
+            (max([now] + [arrival[m] for m in steps[s][1]]), i)
+            for i, s in enumerate(left)
+            if all(n in done for n in steps[s][0]) and all(m in arrival for m in steps[s][1])
+        ]
+        now, i = min(ready)
+        s = left.pop(i)
+        now += steps[s][3]
+        for m, link, kib, hops in steps[s][2]:
+            free[link] = max(free[link], now) + hops * kib / bw
+            arrival[m] = free[link] + lat + hop * (hops - 1)
+        done.add(s)
+        order.append(s)
+    return order
+
+
+def kernel(
+    nz,
+    remote_ref,
+    count_ref,
+    q_ref,
+    k_ref,
+    v_ref,
+    o_ref,
+    g_ref,
+    lse_ref,
+    dq_ref,
+    dk_ref,
+    dv_ref,
+    over_ref,
+    agq0,
+    agq1,
+    agg0,
+    agg1,
+    ags,
+    meta,
+    full,
+    snd,
+    rcv,
+    fwd,
+    psnd,
+    prcv,
+    pfwd,
+    r2snd,
+    r2rcv,
+    r1snd,
+    ret00,
+    ret01,
+    ret10,
+    ret11,
+    own0,
+    own1,
+    rsnd,
+    rrcv,
+    dkacc,
+    dvacc,
+    kt_ref,
+    table,
+    flags,
+    lists,
+    nxt,
+    pos,
+    idx,
+    msk,
+    oidx,
+    omsk,
+    t_sem,
+    z_send,
+    z_recv,
+    y_send,
+    y_recv,
+    f_send,
+    f_recv,
+    r2_send,
+    r2_recv,
+    r1_send,
+    r1_recv,
+    s_send,
+    s_recv,
+):
+    me = lax.axis_index("seq")
+    y = me // nz
+    z = me % nz
+    half = nz // 2
+    cands = 2 * nz
+    scale = float(HD) ** -0.5
+    zdev = [y * nz + lax.rem(z + 1, nz), y * nz + lax.rem(z + nz - 1, nz)]
+    ydev = [lax.rem(y + 1, NY) * nz + z, lax.rem(y + NY - 1, NY) * nz + z]
+    mid = half // 2
+    zfar = [y * nz + lax.rem(z + mid + 1, nz), y * nz + lax.rem(z + nz - mid - 1, nz)]
+    agq = [agq0, agq1]
+    agg = [agg0, agg1]
+    ret = [[ret00, ret01], [ret10, ret11]]
+    own = [own0, own1]
+    chain_refs = [agq0, agg0, agq1, agg1]
+
+    barrier = pltpu.get_barrier_semaphore()
+    for dev in zdev + zfar + ydev:
+        pl.semaphore_signal(
+            barrier, inc=1, device_id={"seq": dev}, device_id_type=pl.DeviceIdType.MESH
+        )
+
+    for h in range(2):
+        cols = slice(h * HD, (h + 1) * HD)
+        for j in range(2):
+            rows = slice(j * BLOCK, (j + 1) * BLOCK)
+            agq[h][2 * z + j] = q_ref[rows, cols]
+            agg[h][2 * z + j] = g_ref[rows, cols]
+            prod = g_ref[rows, cols].astype(F32) * o_ref[rows, cols].astype(F32)
+            ags[z, 4 * h + 2 * j : 4 * h + 2 * j + 1, :] = lse_ref[h : h + 1, rows] * LOG2E
+            ags[z, 4 * h + 2 * j + 1 : 4 * h + 2 * j + 2, :] = jnp.sum(
+                prod.T, axis=0, keepdims=True
+            )
+            ret[h][j][SLOTS] = jnp.zeros((BLOCK, HD), BF16)
+        own[h][OWN] = jnp.zeros((BLOCK, HD), F32)
+        dkacc[h] = jnp.zeros((2 * BLOCK, HD), F32)
+        kt_ref[h] = k_ref[:, cols].T
+        dvacc[h] = jnp.zeros((2 * BLOCK, HD), F32)
+
+    line = lax.broadcasted_iota(I32, (8, BLOCK), 0)
+    lane = lax.broadcasted_iota(I32, (8, BLOCK), 1)
+    rows = jnp.zeros((8, BLOCK), I32)
+    for j in range(2):
+        hit = jnp.where(jnp.abs(lane - (2 * me + j)) <= 1, 1, 0)
+        for r in range(remote_ref.shape[1]):
+            used = jnp.where(count_ref[j] > r, 1, 0)
+            hit = jnp.maximum(hit, jnp.where(lane == remote_ref[j, r], used, 0))
+        rows = jnp.where(line == j, hit, rows)
+    meta[z] = rows
+
+    pl.semaphore_wait(barrier, 6)
+
+    def remote(src, dst, send, recv, dev):
+        return pltpu.make_async_remote_copy(
+            src_ref=src,
+            dst_ref=dst,
+            send_sem=send,
+            recv_sem=recv,
+            device_id={"seq": dev},
+            device_id_type=pl.DeviceIdType.MESH,
+        )
+
+    def z_view(u, j, d, k, at):
+        if u > 3:
+            return (ags, meta)[u - 4].at[at]
+        if j == 2 and k < half:
+            return chain_refs[u].at[pl.ds(2 * at, 2)]
+        return chain_refs[u].at[pl.ds(2 * at + (d if j == 2 else j), 1)]
+
+    def z_copy(u, j, d, k, receiving=False):
+        direct = u > 3 and k == mid + 1
+        hop = k if receiving else 0 if direct else k - 1
+        at = lax.rem(z + nz - hop, nz) if d == 0 else lax.rem(z + hop, nz)
+        view = z_view(u, j, d, k, at)
+        c = CHAINS.index((u, j))
+        sems = z_send.at[c, d, k - 1], z_recv.at[c, d, k - 1]
+        return remote(view, view, *sems, (zfar if direct else zdev)[d])
+
+    def z_step(u, j, d, k):
+        if k > 0:
+            z_copy(u, j, d, k, receiving=True).wait_recv()
+        end = last(u, j, d, half)
+        if k < end and not (u > 3 and k == mid):
+            z_copy(u, j, d, k + 1).start()
+        if k == 0 and u > 3 and mid < end:
+            z_copy(u, j, d, mid + 1).start()
+
+    def z_drain(u):
+        for c, j in CHAINS:
+            if c == u:
+                for d in range(2):
+                    for k in range(1, last(u, j, d, half) + 1):
+                        z_copy(u, j, d, k).wait_send()
+
+    def build_tables():
+        copy = pltpu.make_async_copy(meta, table, t_sem)
+        copy.start()
+        copy.wait()
+
+        def bit(c, yy, b):
+            return table[c // 2, c % 2, lax.rem(y + yy, NY) * cands + 2 * z + b]
+
+        def scan(c, carry):
+            count = []
+            for yy in range(NY):
+                live = bit(c, yy, 0) | bit(c, yy, 1)
+                flags[yy, c] = live
+                count.append(carry[yy] + live)
+            return tuple(count)
+
+        zero = jnp.int32(0)
+        n0, n1p, n2, n1m = lax.fori_loop(0, cands, scan, (zero,) * 4)
+        up = lax.shift_right_arithmetic(n2 + n1m - n1p + 1, jnp.int32(1))
+        up = jnp.minimum(jnp.maximum(up, jnp.maximum(n2 - RELAY, 0)), jnp.minimum(n2, RELAY))
+
+        def place(c, carry):
+            r2, bp, bm, ap, am, ro = carry
+            l0, l1, l2, l3 = flags[0, c], flags[1, c], flags[2, c], flags[3, c]
+            to_p = jnp.where(r2 < up, l2, 0)
+            to_m = l2 - to_p
+            front_p = l1 * (1 - to_p)
+            front_m = l3 * (1 - to_m)
+
+            def where_in(front, a, back, b):
+                p = jnp.where(back > 0, SLOTS - 1 - b, jnp.where(front > 0, a, SLOTS))
+                return jnp.minimum(jnp.maximum(p, 0), SLOTS)
+
+            pos[0, c] = where_in(front_p, ap, to_p, bp)
+            pos[1, c] = where_in(front_m, am, to_m, bm)
+            pos[2, c] = jnp.minimum(jnp.where(l0 > 0, ro, OWN), OWN)
+            lists[0, c] = front_p
+            lists[1, c] = to_p
+            lists[2, c] = front_m
+            lists[3, c] = to_m
+            lists[4, c] = l0
+            return r2 + l2, bp + to_p, bm + to_m, ap + front_p, am + front_m, ro + l0
+
+        _, bp, bm, ap, am, _ = lax.fori_loop(0, cands, place, (zero,) * 6)
+        most = jnp.maximum(jnp.maximum(ap + bp, am + bm) - SLOTS, n0 - OWN)
+        most = jnp.maximum(most, jnp.maximum(bp, bm) - RELAY)
+        full[...] = jnp.broadcast_to(jnp.where(most > 0, 1.0, 0.0).astype(F32), (8, BLOCK))
+
+        for n in range(5):
+            nxt[n, cands] = jnp.int32(cands)
+            nxt[n, cands + 1] = jnp.int32(cands)
+
+        def back(i, carry):
+            c = cands - 1 - i
+            out = []
+            for n in range(5):
+                cur = jnp.where(lists[n, c] > 0, c, carry[n])
+                nxt[n, c] = cur
+                out.append(cur)
+            return tuple(out)
+
+        lax.fori_loop(0, cands, back, (jnp.int32(cands),) * 5)
+
+        for d in range(2):
+            front = nxt[2 * d, 0]
+            fronts = []
+            for p in range(SLOTS):
+                fronts.append(front)
+                front = nxt[2 * d, front + 1]
+            tail = nxt[2 * d + 1, 0]
+            tails = []
+            for p in range(RELAY):
+                tails.append(tail)
+                tail = nxt[2 * d + 1, tail + 1]
+            for p in range(SLOTS):
+                c = fronts[p]
+                live2 = jnp.int32(0)
+                if p >= SLOTS - RELAY:
+                    t = tails[SLOTS - 1 - p]
+                    live2 = jnp.where(t < cands, 1, 0)
+                    c = jnp.where(t < cands, t, c)
+                live1 = jnp.where(c < cands, 1, 0)
+                c = jnp.minimum(c, cands - 1)
+                idx[d, p] = c
+                yy = 1 if d == 0 else NY - 1
+                msk[d, p, 0] = live1 * bit(c, yy, 0)
+                msk[d, p, 1] = live1 * bit(c, yy, 1)
+                msk[d, p, 2] = live2 * bit(c, 2, 0)
+                msk[d, p, 3] = live2 * bit(c, 2, 1)
+        cur = nxt[4, 0]
+        for p in range(OWN):
+            c = jnp.minimum(cur, cands - 1)
+            live = jnp.where(cur < cands, 1, 0)
+            oidx[p] = c
+            omsk[0, p] = live * bit(c, 0, 0)
+            omsk[1, p] = live * bit(c, 0, 1)
+            if p + 1 < OWN:
+                cur = nxt[4, cur + 1]
+
+    def pairs(h, queries, grads, lse0, lse1, delta):
+        cols = slice(h * HD, (h + 1) * HD)
+        scores = dot(k_ref[:, cols], queries, 1, 1) * (scale * LOG2E)
+        weights = jnp.concatenate(
+            [jnp.exp2(scores[:BLOCK] - lse0), jnp.exp2(scores[BLOCK:] - lse1)], axis=0
+        )
+        dvacc[h] += dot(weights.astype(BF16), grads, 1, 0)
+        grad_probs = dot(v_ref[:, cols], grads, 1, 1)
+        grad_scores = (weights * (grad_probs - delta)).astype(BF16)
+        dkacc[h] += dot(grad_scores, queries, 1, 0)
+        return dot(kt_ref[h], grad_scores, 1, 0) * scale
+
+    def stat_rows(h, c):
+        tile = ags[c // 2]
+        odd = c % 2 > 0
+        lse = jnp.where(odd, tile[4 * h + 2 : 4 * h + 3], tile[4 * h : 4 * h + 1])
+        delta = jnp.where(odd, tile[4 * h + 3 : 4 * h + 4], tile[4 * h + 1 : 4 * h + 2])
+        return lse, delta
+
+    def join(parts, axis):
+        return jnp.concatenate(parts, axis=axis)
+
+    def own_pairs(h, lo, hi):
+        qs, gs, l0, l1, dl = [], [], [], [], []
+        for p in range(lo, hi):
+            c = oidx[p]
+            lse, delta = stat_rows(h, c)
+            qs.append(agq[h][c])
+            gs.append(agg[h][c])
+            l0.append(jnp.where(omsk[0, p] > 0, lse, DEAD))
+            l1.append(jnp.where(omsk[1, p] > 0, lse, DEAD))
+            dl.append(delta)
+        got = pairs(h, join(qs, 0), join(gs, 0), join(l0, 1), join(l1, 1), join(dl, 1))
+        for p in range(lo, hi):
+            own[h][p] = got[:, (p - lo) * BLOCK : (p - lo + 1) * BLOCK]
+
+    def packet_pairs(h, d, blocks, stats, row, lo, hi, put):
+        queries = blocks[h, 0, d, lo:hi].reshape((hi - lo) * BLOCK, HD)
+        grads = blocks[h, 1, d, lo:hi].reshape((hi - lo) * BLOCK, HD)
+
+        def rows(r):
+            return join([stats[h, d, p][r : r + 1] for p in range(lo, hi)], 1)
+
+        got = pairs(h, queries, grads, rows(row), rows(row + 1), rows(4))
+        for p in range(lo, hi):
+            put(p, got[:, (p - lo) * BLOCK : (p - lo + 1) * BLOCK])
+
+    def pack(h, t, d):
+        if t < 2:
+            source = (agq, agg)[t][h]
+
+            for part in (1, 0):
+                @pl.loop(FRONT * part, SLOTS if part else FRONT)
+                def _(p):
+                    snd[h, t, d, p] = source[idx[d, p]]
+
+                y_copy(h, t, d, part).start()
+        else:
+            @pl.loop(0, SLOTS)
+            def _(p):
+                lse, delta = stat_rows(h, idx[d, p])
+                tile = jnp.where(line == 4, delta, 0.0)
+                tile = jnp.where(line == 5, full[0:1], tile)
+                for r in range(4):
+                    row = jnp.where(msk[d, p, r] > 0, lse, DEAD)
+                    tile = jnp.where(line == r, row, tile)
+                psnd[h, d, p] = tile
+
+            y_copy(h, t, d, 1).start()
+
+    def y_copy(h, t, d, part):
+        at = pl.ds(FRONT, RELAY) if part else pl.ds(0, FRONT)
+        if t == 2:
+            src, dst = psnd.at[h, d], prcv.at[h, d]
+        else:
+            src, dst = snd.at[h, t, d, at], rcv.at[h, t, d, at]
+        return remote(src, dst, y_send.at[h, t, d, part], y_recv.at[h, t, d, part], ydev[d])
+
+    def f_copy(h, t, d):
+        last = pl.ds(SLOTS - RELAY, RELAY)
+        if t == 2:
+            src, dst = prcv.at[h, d, last], pfwd.at[h, d]
+        else:
+            src, dst = rcv.at[h, t, d, last], fwd.at[h, t, d]
+        return remote(src, dst, f_send.at[h, t, d], f_recv.at[h, t, d], ydev[d])
+
+    def relay(h, t, d):
+        y_copy(h, t, d, 1).wait_recv()
+        f_copy(h, t, d).start()
+
+    def r2_copy(h, d):
+        return remote(
+            r2snd.at[h, d], r2rcv.at[h, d], r2_send.at[h, d], r2_recv.at[h, d], ydev[1 - d]
+        )
+
+    def r1_copy(h, d, part):
+        at = pl.ds(0, SLOTS - RELAY) if part == 0 else pl.ds(SLOTS - RELAY, RELAY)
+        return remote(
+            r1snd.at[h, d, at],
+            ret[h][d].at[at],
+            r1_send.at[h, d, part],
+            r1_recv.at[h, d, part],
+            ydev[1 - d],
+        )
+
+    def far_pairs(h, d):
+        for t in range(3):
+            f_copy(h, t, d).wait_recv()
+
+        def put(p, got):
+            r2snd[h, d, p] = got.astype(BF16)
+
+        packet_pairs(h, d, fwd, pfwd, 2, 0, RELAY, put)
+        r2_copy(h, d).start()
+
+    def near_pairs(h, d):
+        for t in range(2):
+            y_copy(h, t, d, 0).wait_recv()
+
+        def put(p, got):
+            r1snd[h, d, p] = got.astype(BF16)
+
+        packet_pairs(h, d, rcv, prcv, 0, 0, SLOTS - RELAY, put)
+        r1_copy(h, d, 0).start()
+
+    def relay_pairs(h, d):
+        r2_copy(h, d).wait_recv()
+
+        def put(p, got):
+            back = r2rcv[h, d, p - (SLOTS - RELAY)].astype(F32)
+            r1snd[h, d, p] = (got + back).astype(BF16)
+
+        packet_pairs(h, d, rcv, prcv, 0, SLOTS - RELAY, SLOTS, put)
+        r1_copy(h, d, 1).start()
+
+    def terms(h, at, j):
+        c = 2 * at + j
+        total = own[h][pos[2, c]]
+        for d in range(2):
+            total = total + ret[h][d][pos[d, c]].astype(F32)
+        return total
+
+    def s_copy(h, d, j, k):
+        at = pl.ds(0, BLOCK + 16 if h == 0 and j == d else BLOCK)
+        return remote(
+            rsnd.at[h, d, j, k - 1, at],
+            rrcv.at[h, d, j, k - 1, at],
+            s_send.at[h, d, j, k - 1],
+            s_recv.at[h, d, j, k - 1],
+            (zfar if k == mid else zdev)[1 - d],
+        )
+
+    extra = slice(BLOCK, BLOCK + 16)
+
+    def s_step(h, d, j, k):
+        dist = half + 1 - k
+        at = lax.rem(z + nz - dist, nz) if d == 0 else lax.rem(z + dist, nz)
+        total = terms(h, at, j)
+        carries = h == 0 and j == d
+        if carries:
+            rsnd[h, d, j, k - 1, extra] = jnp.broadcast_to(full[0:1], (16, HD)).astype(BF16)
+        if k != mid + 1 and (k > 2 or (k == 2 and j == d)):
+            s_copy(h, d, j, k - 1).wait_recv()
+            total = total + rrcv[h, d, j, k - 2, :BLOCK].astype(F32)
+            if carries:
+                rsnd[h, d, j, k - 1, extra] = jnp.maximum(
+                    rsnd[h, d, j, k - 1, extra], rrcv[h, d, j, k - 2, extra]
+                )
+        rsnd[h, d, j, k - 1, :BLOCK] = total.astype(BF16)
+        s_copy(h, d, j, k).start()
+        if k - 2 >= (mid + 1 if k > mid else 1 if j == d else 2):
+            s_copy(h, d, j, k - 2).wait_send()
+
+    def s_end(h):
+        cols = slice(h * HD, (h + 1) * HD)
+        any_full = full[0:1]
+        for j in range(2):
+            total = terms(h, z, j)
+            for d in range(2):
+                for k in (mid, half):
+                    if k > 1 or j == d:
+                        s_copy(h, d, j, k).wait_recv()
+                        total = total + rrcv[h, d, j, k - 1, :BLOCK].astype(F32)
+                        if h == 0 and j == d:
+                            got = rrcv[h, d, j, k - 1, extra].astype(F32)
+                            any_full = jnp.maximum(any_full, got[0:1])
+                for lo, hi in ((1 if j == d else 2, mid), (mid + 1, half)):
+                    for k in range(max(lo, hi - 1), hi + 1):
+                        s_copy(h, d, j, k).wait_send()
+            dq_ref[j * BLOCK : (j + 1) * BLOCK, cols] = total.T.astype(BF16)
+        if h == 0:
+            over_ref[...] = jnp.broadcast_to(any_full, (8, BLOCK))
+
+    def r1_wait(h):
+        for d in range(2):
+            for part in range(2):
+                r1_copy(h, d, part).wait_recv()
+        if h == 0:
+            seen = full[0:1]
+            for d in range(2):
+                seen = jnp.maximum(seen, jnp.maximum(prcv[0, d, 0][5:6], pfwd[0, d, 0][5:6]))
+            full[...] = jnp.broadcast_to(seen, (8, BLOCK))
+
+    def results(h):
+        cols = slice(h * HD, (h + 1) * HD)
+        dk_ref[:, cols] = (dkacc[h] * scale).astype(BF16)
+        dv_ref[:, cols] = dvacc[h].astype(BF16)
+
+    def y_drain(h):
+        for d in range(2):
+            for t in range(3):
+                for part in range(2):
+                    if t < 2 or part:
+                        y_copy(h, t, d, part).wait_send()
+                f_copy(h, t, d).wait_send()
+            r2_copy(h, d).wait_send()
+            for part in range(2):
+                r1_copy(h, d, part).wait_send()
+
+    do = {
+        "z": z_step,
+        "tab": build_tables,
+        "own": lambda h, i: own_pairs(h, 4 * i, 4 * i + 4),
+        "pk": pack,
+        "f": relay,
+        "far": far_pairs,
+        "na": near_pairs,
+        "nb": relay_pairs,
+        "w": r1_wait,
+        "kv": results,
+        "zq": z_drain,
+        "yq": y_drain,
+        "s": s_step,
+        "e": s_end,
+    }
+    for step in plan(half):
+        do[step[0]](*step[1:])
+
+
+def fast(nz, remote, count, query, key, value, output, grad_out, logsumexp):
+    rows, width = query.shape
+    half = nz // 2
+    blocks = (2 * nz, BLOCK, HD)
+    vmem, dma = pltpu.VMEM, pltpu.SemaphoreType.DMA
+    smem = pltpu.SMEM
+    outs = [jax.ShapeDtypeStruct((rows, width), BF16)] * 3
+    outs.append(jax.ShapeDtypeStruct((8, BLOCK), F32))
+    in_vmem = pl.BlockSpec(memory_space=pltpu.VMEM)
+    scratch = [
+        *[vmem(blocks, BF16)] * 4,
+        vmem((nz, 8, BLOCK), F32),
+        vmem((nz, 8, BLOCK), I32),
+        vmem((8, BLOCK), F32),
+        vmem((2, 2, 2, SLOTS, BLOCK, HD), BF16),
+        vmem((2, 2, 2, SLOTS, BLOCK, HD), BF16),
+        vmem((2, 2, 2, RELAY, BLOCK, HD), BF16),
+        vmem((2, 2, SLOTS, 8, BLOCK), F32),
+        vmem((2, 2, SLOTS, 8, BLOCK), F32),
+        vmem((2, 2, RELAY, 8, BLOCK), F32),
+        vmem((2, 2, RELAY, BLOCK, HD), BF16),
+        vmem((2, 2, RELAY, BLOCK, HD), BF16),
+        vmem((2, 2, SLOTS, BLOCK, HD), BF16),
+        *[vmem((SLOTS + 1, BLOCK, HD), BF16)] * 4,
+        *[vmem((OWN + 1, BLOCK, HD), F32)] * 2,
+        vmem((2, 2, 2, half, BLOCK + 16, HD), BF16),
+        vmem((2, 2, 2, half, BLOCK + 16, HD), BF16),
+        vmem((2, 2 * BLOCK, HD), F32),
+        vmem((2, 2 * BLOCK, HD), F32),
+        vmem((2, HD, 2 * BLOCK), BF16),
+        smem((nz, 8, BLOCK), I32),
+        smem((NY, 2 * nz), I32),
+        smem((5, 2 * nz), I32),
+        smem((5, 2 * nz + 2), I32),
+        smem((3, 2 * nz), I32),
+        smem((2, SLOTS), I32),
+        smem((2, SLOTS, 4), I32),
+        smem((OWN,), I32),
+        smem((2, OWN), I32),
+        pltpu.SemaphoreType.DMA,
+        *[dma((len(CHAINS), 2, half))] * 2,
+        *[dma((2, 3, 2, 2))] * 2,
+        *[dma((2, 3, 2))] * 2,
+        *[dma((2, 2))] * 2,
+        *[dma((2, 2, 2))] * 2,
+        *[dma((2, 2, 2, half))] * 2,
+    ]
+    return pl.pallas_call(
+        functools.partial(kernel, nz),
+        out_shape=outs,
+        in_specs=[pl.BlockSpec(memory_space=pltpu.SMEM)] * 2 + [in_vmem] * 6,
+        out_specs=[in_vmem] * 4,
+        scratch_shapes=scratch,
+        compiler_params=pltpu.CompilerParams(
+            collective_id=0, has_side_effects=True, vmem_limit_bytes=48 * 1024 * 1024
+        ),
+        cost_estimate=pl.CostEstimate(
+            flops=4 * 10**9, bytes_accessed=4 * 2**20, transcendentals=5 * 10**6
+        ),
+    )(remote, count, query, key, value, output, grad_out, logsumexp)
+
+
+def per_device(query, key, value, output, grad_out, logsumexp, remote_blocks, remote_count):
+    nz = lax.axis_size("seq") // NY
+    *found, over = fast(
+        nz, remote_blocks, remote_count, query, key, value, output, grad_out, logsumexp
+    )
+    return lax.cond(
+        over[0, 0] > 0,
+        lambda: general(
+            query, key, value, output, grad_out, logsumexp, remote_blocks, remote_count
+        ),
+        lambda: tuple(found),
     )
 
 

time: 826 us -> 139 us (0.17)
  the two profiles are of different devices: /device:TPU:24 before, /device:TPU:2 now
where the time goes in v1:
time: 139 us
  Pallas kernels  135 us (97%)
  local copies, waits for them, and re-layouts  2.51 us (2%)
  between operations  1.43 us (1%)
    pallas_call x1, Pallas kernels, fast(): pl.pallas_call(functools.partial(kernel, nz), out_shape=outs, in_specs=[p...  135 us

profile of v1, /device:TPU:2, one launch (start us, length us, event | category | flops | bytes accessed | tf_op | source)
XLA Modules:
  0.0 139.2 jit_solution(993049110709719702)
XLA Ops:
  0.6 0.0 copy-start.8
  0.6 0.0 copy-start.6
  0.7 0.0 copy-start.5
  0.7 0.0 copy-start.2
  0.7 0.0 copy-start.4
  0.7 0.0 copy-start.1
  0.7 0.0 copy-start
  0.7 0.0 copy-start.3
  0.7 135.0 %shard_map.109 = (bf16[256,256]{1,0:T(8,128)(2,1)S(1)}, bf16[256,256]{1,0:T(8,128)(2,1)S(1)}, bf16[256,256]{1,0:T(8,128)(2,1)S(1)}, f32[8,128]{1,0:T(8,128)S(1)}) custom-call(s32[2,8]{1,0:T(2,128)} %remote_ref.1, s32[2]{0:T(128)} %count_ref.1, bf16[256,256]{1,0:T(8,128)(2,1)} %q_ref.1, bf16[256,256]{1,0:T(8,128)(2,1)} %k_ref.1, bf16[256,256]{1,0:T(8,128)(2,1)} %v_ref.1, ...), custom_call_target="tpu_custom_call" | custom-call | flops 4000000000 | bytes 4194304 | tf_op jit(solution)/shard_map/pallas_call | solution.py:870
  135.7 0.5 slice.141
  136.9 0.0 copy-done.8
  136.9 0.0 copy-done.6
  136.9 0.0 copy-done.5
  136.9 0.0 copy-done.2
  136.9 0.0 copy-done.4
  137.0 0.0 copy-done.1
  137.0 0.0 copy-done
  137.0 0.0 copy-done.3
  137.0 0.3 conditional.1
  137.3 0.7 copy.284
  137.9 0.7 copy.285
  138.6 0.7 copy.286
Async XLA Ops:
  0.6 136.3 %copy-start.8 = (s32[2]{0:T(128)S(1)}, s32[2]{0:T(128)}, u32[]{:S(2)}) copy-start(s32[2]{0:T(128)} %count_ref.1) | copy-start | bytes 28
  0.6 136.3 %copy-start.6 = (s32[2,8]{1,0:T(2,128)S(1)}, s32[2,8]{1,0:T(2,128)}, u32[]{:S(2)}) copy-start(s32[2,8]{1,0:T(2,128)} %remote_ref.1) | copy-start | bytes 196
  0.7 136.3 %copy-start.5 = (f32[2,256]{1,0:T(2,128)S(1)}, f32[2,256]{1,0:T(2,128)}, u32[]{:S(2)}) copy-start(f32[2,256]{1,0:T(2,128)} %lse_ref.1) | copy-start | bytes 6148
  0.7 136.3 %copy-start.2 = (bf16[256,256]{1,0:T(8,128)(2,1)S(1)}, bf16[256,256]{1,0:T(8,128)(2,1)}, u32[]{:S(2)}) copy-start(bf16[256,256]{1,0:T(8,128)(2,1)} %g_ref.1) | copy-start | bytes 393220
  0.7 136.3 %copy-start.4 = (bf16[256,256]{1,0:T(8,128)(2,1)S(1)}, bf16[256,256]{1,0:T(8,128)(2,1)}, u32[]{:S(2)}) copy-start(bf16[256,256]{1,0:T(8,128)(2,1)} %o_ref.1) | copy-start | bytes 393220
  0.7 136.3 %copy-start.1 = (bf16[256,256]{1,0:T(8,128)(2,1)S(1)}, bf16[256,256]{1,0:T(8,128)(2,1)}, u32[]{:S(2)}) copy-start(bf16[256,256]{1,0:T(8,128)(2,1)} %v_ref.1) | copy-start | bytes 393220
  0.7 136.3 %copy-start = (bf16[256,256]{1,0:T(8,128)(2,1)S(1)}, bf16[256,256]{1,0:T(8,128)(2,1)}, u32[]{:S(2)}) copy-start(bf16[256,256]{1,0:T(8,128)(2,1)} %k_ref.1) | copy-start | bytes 393220
  0.7 136.3 %copy-start.3 = (bf16[256,256]{1,0:T(8,128)(2,1)S(1)}, bf16[256,256]{1,0:T(8,128)(2,1)}, u32[]{:S(2)}) copy-start(bf16[256,256]{1,0:T(8,128)(2,1)} %q_ref.1) | copy-start | bytes 393220

commit v2 on v1

--- a/solution.py
+++ b/solution.py
@@ -204,7 +204,7 @@
     return lax.dot_general(a, b, (((ca,), (cb,)), ((), ())), preferred_element_type=F32)
 
 
-FINE = (0, 1)
+FINE = ()
 CHAINS = [(u, j) for u in range(6) for j in ((0, 1) if u in FINE else (2,))]
 
 
@@ -214,7 +214,7 @@
     return half if u < 4 or d == 0 else half - 1
 
 
-def plan(half, release=(0, 7, 3), lat=2.0, chunk=0.35, tab=4.0, bw=51.2, hop=0.3, iss=0.1):
+def plan(half, release=(0, 1, 4), lat=2.1, chunk=0.4, tab=4.0, bw=75.0, hop=0.3, iss=0.15):
     F, R = SLOTS, RELAY
     mid = half // 2
     steps = {}
@@ -274,18 +274,16 @@
         steps["kv", h] = (pairs, [], [], 0.2)
         fin = []
         for d in range(2):
-            for j in range(2):
-                for k in range(1, half + 1):
-                    if k > 1 or j == d:
-                        first = k == 1 or (k == 2 and j != d) or k == mid + 1
-                        awaits = [] if first else [("s", h, d, j, k - 1)]
-                        hops = mid + 1 if k == mid else 1
-                        if k in (mid, half):
-                            fin.append(("s", h, d, j, k))
-                        steps["s", h, d, j, k] = ([("w", h)], awaits, [(("s", h, d, j, k), 1 - d, 32, hops)], 0.12)
+            for k in range(1, half + 1):
+                awaits = [] if k in (1, mid + 1) else [("s", h, d, k - 1)]
+                hops = mid + 1 if k == mid else 1
+                if k in (mid, half):
+                    fin.append(("s", h, d, k))
+                sends = [(("s", h, d, k), 1 - d, 68 if k > 1 else 36, hops)]
+                steps["s", h, d, k] = ([("w", h)], awaits, sends, 0.25)
         for t in range(2):
             steps["zq", 2 * h + t] = (got[t] + [("pk", h, t, 1)], [], [], 0.5)
-        steps["yq", h] = ([("s", h, 0, 0, half // 2 + 1)], [], [], 0.5)
+        steps["yq", h] = ([("s", h, 0, half // 2 + 1)], [], [], 0.5)
         steps["e", h] = ([("w", h)], fin, [], 0.3)
     for s in list(steps):
         n, a, sd, c = steps[s]
@@ -317,8 +315,9 @@
         s = left.pop(i)
         now += steps[s][3]
         for m, link, kib, hops in steps[s][2]:
-            free[link] = max(free[link], now) + hops * kib / bw
-            arrival[m] = free[link] + lat + hop * (hops - 1)
+            begin = max(free[link], now)
+            free[link] = begin + hops * kib / bw
+            arrival[m] = begin + min(hops, 2) * kib / bw + lat + hop * (hops - 1)
         done.add(s)
         order.append(s)
     return order
@@ -410,34 +409,44 @@
             barrier, inc=1, device_id={"seq": dev}, device_id_type=pl.DeviceIdType.MESH
         )
 
-    for h in range(2):
-        cols = slice(h * HD, (h + 1) * HD)
+    def put_blocks(ref, own_ref, h):
         for j in range(2):
-            rows = slice(j * BLOCK, (j + 1) * BLOCK)
-            agq[h][2 * z + j] = q_ref[rows, cols]
-            agg[h][2 * z + j] = g_ref[rows, cols]
-            prod = g_ref[rows, cols].astype(F32) * o_ref[rows, cols].astype(F32)
-            ags[z, 4 * h + 2 * j : 4 * h + 2 * j + 1, :] = lse_ref[h : h + 1, rows] * LOG2E
-            ags[z, 4 * h + 2 * j + 1 : 4 * h + 2 * j + 2, :] = jnp.sum(
-                prod.T, axis=0, keepdims=True
-            )
-            ret[h][j][SLOTS] = jnp.zeros((BLOCK, HD), BF16)
-        own[h][OWN] = jnp.zeros((BLOCK, HD), F32)
-        dkacc[h] = jnp.zeros((2 * BLOCK, HD), F32)
-        kt_ref[h] = k_ref[:, cols].T
-        dvacc[h] = jnp.zeros((2 * BLOCK, HD), F32)
+            ref[2 * z + j] = own_ref[j * BLOCK : (j + 1) * BLOCK, h * HD : (h + 1) * HD]
 
     line = lax.broadcasted_iota(I32, (8, BLOCK), 0)
     lane = lax.broadcasted_iota(I32, (8, BLOCK), 1)
-    rows = jnp.zeros((8, BLOCK), I32)
-    for j in range(2):
-        hit = jnp.where(jnp.abs(lane - (2 * me + j)) <= 1, 1, 0)
-        for r in range(remote_ref.shape[1]):
-            used = jnp.where(count_ref[j] > r, 1, 0)
-            hit = jnp.maximum(hit, jnp.where(lane == remote_ref[j, r], used, 0))
-        rows = jnp.where(line == j, hit, rows)
-    meta[z] = rows
-
+
+    def put_rows():
+        rows = jnp.zeros((8, BLOCK), I32)
+        for j in range(2):
+            hit = jnp.where(jnp.abs(lane - (2 * me + j)) <= 1, 1, 0)
+            for r in range(remote_ref.shape[1]):
+                used = jnp.where(count_ref[j] > r, 1, 0)
+                hit = jnp.maximum(hit, jnp.where(lane == remote_ref[j, r], used, 0))
+            rows = jnp.where(line == j, hit, rows)
+        meta[z] = rows
+
+    def put_stats():
+        for h in range(2):
+            cols = slice(h * HD, (h + 1) * HD)
+            for j in range(2):
+                rows = slice(j * BLOCK, (j + 1) * BLOCK)
+                prod = g_ref[rows, cols].astype(F32) * o_ref[rows, cols].astype(F32)
+                at = 4 * h + 2 * j
+                ags[z, at : at + 1, :] = lse_ref[h : h + 1, rows] * LOG2E
+                ags[z, at + 1 : at + 2, :] = jnp.sum(prod.T, axis=0, keepdims=True)
+
+    def put_rest():
+        for h in range(2):
+            for d in range(2):
+                ret[h][d][SLOTS] = jnp.zeros((BLOCK, HD), BF16)
+            own[h][OWN] = jnp.zeros((BLOCK, HD), F32)
+            dkacc[h] = jnp.zeros((2 * BLOCK, HD), F32)
+            dvacc[h] = jnp.zeros((2 * BLOCK, HD), F32)
+            kt_ref[h] = k_ref[:, h * HD : (h + 1) * HD].T
+
+    put_blocks(agq[0], q_ref, 0)
+    put_rows()
     pl.semaphore_wait(barrier, 6)
 
     def remote(src, dst, send, recv, dev):
@@ -723,54 +732,59 @@
             total = total + ret[h][d][pos[d, c]].astype(F32)
         return total
 
-    def s_copy(h, d, j, k):
-        at = pl.ds(0, BLOCK + 16 if h == 0 and j == d else BLOCK)
+    block_rows = (slice(0, BLOCK), slice(BLOCK + 16, 2 * BLOCK + 16))
+    flag_rows = slice(BLOCK, BLOCK + 16)
+
+    def s_copy(h, d, k):
+        at = pl.ds(0, 2 * BLOCK + 16)
+        if k == 1:
+            at = pl.ds(BLOCK * d, BLOCK + 16)
         return remote(
-            rsnd.at[h, d, j, k - 1, at],
-            rrcv.at[h, d, j, k - 1, at],
-            s_send.at[h, d, j, k - 1],
-            s_recv.at[h, d, j, k - 1],
+            rsnd.at[h, d, k - 1, at],
+            rrcv.at[h, d, k - 1, at],
+            s_send.at[h, d, k - 1],
+            s_recv.at[h, d, k - 1],
             (zfar if k == mid else zdev)[1 - d],
         )
 
-    extra = slice(BLOCK, BLOCK + 16)
-
-    def s_step(h, d, j, k):
+    def s_has(d, j, k):
+        return k > 1 or j == d
+
+    def s_step(h, d, k):
         dist = half + 1 - k
         at = lax.rem(z + nz - dist, nz) if d == 0 else lax.rem(z + dist, nz)
-        total = terms(h, at, j)
-        carries = h == 0 and j == d
-        if carries:
-            rsnd[h, d, j, k - 1, extra] = jnp.broadcast_to(full[0:1], (16, HD)).astype(BF16)
-        if k != mid + 1 and (k > 2 or (k == 2 and j == d)):
-            s_copy(h, d, j, k - 1).wait_recv()
-            total = total + rrcv[h, d, j, k - 2, :BLOCK].astype(F32)
-            if carries:
-                rsnd[h, d, j, k - 1, extra] = jnp.maximum(
-                    rsnd[h, d, j, k - 1, extra], rrcv[h, d, j, k - 2, extra]
-                )
-        rsnd[h, d, j, k - 1, :BLOCK] = total.astype(BF16)
-        s_copy(h, d, j, k).start()
-        if k - 2 >= (mid + 1 if k > mid else 1 if j == d else 2):
-            s_copy(h, d, j, k - 2).wait_send()
+        flag = jnp.broadcast_to(full[0:1], (16, HD)).astype(BF16)
+        total = {j: terms(h, at, j) for j in range(2) if s_has(d, j, k)}
+        if k not in (1, mid + 1):
+            s_copy(h, d, k - 1).wait_recv()
+            flag = jnp.maximum(flag, rrcv[h, d, k - 2, flag_rows])
+            for j in range(2):
+                if s_has(d, j, k - 1):
+                    total[j] = total[j] + rrcv[h, d, k - 2, block_rows[j]].astype(F32)
+        for j in total:
+            rsnd[h, d, k - 1, block_rows[j]] = total[j].astype(BF16)
+        rsnd[h, d, k - 1, flag_rows] = flag
+        s_copy(h, d, k).start()
+        if k - 2 >= (mid + 1 if k > mid else 1):
+            s_copy(h, d, k - 2).wait_send()
 
     def s_end(h):
         cols = slice(h * HD, (h + 1) * HD)
         any_full = full[0:1]
+        total = [terms(h, z, j) for j in range(2)]
+        for d in range(2):
+            for k in (mid, half):
+                s_copy(h, d, k).wait_recv()
+                got = rrcv[h, d, k - 1, flag_rows].astype(F32)
+                any_full = jnp.maximum(any_full, got[0:1])
+                for j in range(2):
+                    if s_has(d, j, k):
+                        total[j] = total[j] + rrcv[h, d, k - 1, block_rows[j]].astype(F32)
+            for lo, hi in ((1, mid), (mid + 1, half)):
+                for k in range(max(lo, hi - 1), hi + 1):
+                    s_copy(h, d, k).wait_send()
         for j in range(2):
-            total = terms(h, z, j)
-            for d in range(2):
-                for k in (mid, half):
-                    if k > 1 or j == d:
-                        s_copy(h, d, j, k).wait_recv()
-                        total = total + rrcv[h, d, j, k - 1, :BLOCK].astype(F32)
-                        if h == 0 and j == d:
-                            got = rrcv[h, d, j, k - 1, extra].astype(F32)
-                            any_full = jnp.maximum(any_full, got[0:1])
-                for lo, hi in ((1 if j == d else 2, mid), (mid + 1, half)):
-                    for k in range(max(lo, hi - 1), hi + 1):
-                        s_copy(h, d, j, k).wait_send()
-            dq_ref[j * BLOCK : (j + 1) * BLOCK, cols] = total.T.astype(BF16)
+            dq_ref[j * BLOCK : (j + 1) * BLOCK, cols] = total[j].T.astype(BF16)
         if h == 0:
             over_ref[...] = jnp.broadcast_to(any_full, (8, BLOCK))
 
@@ -816,8 +830,17 @@
         "s": s_step,
         "e": s_end,
     }
-    for step in plan(half):
+    steps = plan(half)
+    ahead = [("z", 0, 2, d, 0) for d in range(2)]
+    for step in ahead:
         do[step[0]](*step[1:])
+    put_stats()
+    for u in range(1, 4):
+        put_blocks(chain_refs[u], (q_ref, g_ref)[u % 2], u // 2)
+    put_rest()
+    for step in steps:
+        if step not in ahead:
+            do[step[0]](*step[1:])
 
 
 def fast(nz, remote, count, query, key, value, output, grad_out, logsumexp):
@@ -845,8 +868,8 @@
         vmem((2, 2, SLOTS, BLOCK, HD), BF16),
         *[vmem((SLOTS + 1, BLOCK, HD), BF16)] * 4,
         *[vmem((OWN + 1, BLOCK, HD), F32)] * 2,
-        vmem((2, 2, 2, half, BLOCK + 16, HD), BF16),
-        vmem((2, 2, 2, half, BLOCK + 16, HD), BF16),
+        vmem((2, 2, half, 2 * BLOCK + 16, HD), BF16),
+        vmem((2, 2, half, 2 * BLOCK + 16, HD), BF16),
         vmem((2, 2 * BLOCK, HD), F32),
         vmem((2, 2 * BLOCK, HD), F32),
         vmem((2, HD, 2 * BLOCK), BF16),
@@ -865,7 +888,7 @@
         *[dma((2, 3, 2))] * 2,
         *[dma((2, 2))] * 2,
         *[dma((2, 2, 2))] * 2,
-        *[dma((2, 2, 2, half))] * 2,
+        *[dma((2, 2, half))] * 2,
     ]
     return pl.pallas_call(
         functools.partial(kernel, nz),

time: 139 us -> 155 us (1.12)
  the two profiles are of different devices: /device:TPU:2 before, /device:TPU:24 now
where the time goes in v2:
time: 155 us; the launch traced here: 153 us
  Pallas kernels  148 us (95%)
  local copies, waits for them, and re-layouts  2.51 us (2%)
    pallas_call x1, Pallas kernels, fast(): pl.pallas_call(functools.partial(kernel, nz), out_shape=outs, in_specs=[p...  148 us

profile of v2, /device:TPU:24, one launch (start us, length us, event | category | flops | bytes accessed | tf_op | source)
XLA Modules:
  0.0 152.6 jit_solution(9883340743038860973)
XLA Ops:
  0.6 0.0 copy-start.8
  0.6 0.0 copy-start.6
  0.7 0.0 copy-start.5
  0.7 0.0 copy-start.2
  0.7 0.0 copy-start.4
  0.7 0.0 copy-start.1
  0.7 0.0 copy-start
  0.7 0.0 copy-start.3
  0.7 148.5 %shard_map.109 = (bf16[256,256]{1,0:T(8,128)(2,1)S(1)}, bf16[256,256]{1,0:T(8,128)(2,1)S(1)}, bf16[256,256]{1,0:T(8,128)(2,1)S(1)}, f32[8,128]{1,0:T(8,128)S(1)}) custom-call(s32[2,8]{1,0:T(2,128)} %remote_ref.1, s32[2]{0:T(128)} %count_ref.1, bf16[256,256]{1,0:T(8,128)(2,1)} %q_ref.1, bf16[256,256]{1,0:T(8,128)(2,1)} %k_ref.1, bf16[256,256]{1,0:T(8,128)(2,1)} %v_ref.1, ...), custom_call_target="tpu_custom_call" | custom-call | flops 4000000000 | bytes 4194304 | tf_op jit(solution)/shard_map/pallas_call | solution.py:893
  149.2 0.5 slice.141
  150.4 0.0 copy-done.8
  150.4 0.0 copy-done.6
  150.4 0.0 copy-done.5
  150.4 0.0 copy-done.2
  150.4 0.0 copy-done.4
  150.4 0.0 copy-done.1
  150.4 0.0 copy-done
  150.4 0.0 copy-done.3
  150.4 0.2 conditional.1
  150.7 0.7 copy.284
  151.3 0.7 copy.285
  152.0 0.7 copy.286
Async XLA Ops:
  0.6 149.7 %copy-start.8 = (s32[2]{0:T(128)S(1)}, s32[2]{0:T(128)}, u32[]{:S(2)}) copy-start(s32[2]{0:T(128)} %count_ref.1) | copy-start | bytes 28
  0.6 149.7 %copy-start.6 = (s32[2,8]{1,0:T(2,128)S(1)}, s32[2,8]{1,0:T(2,128)}, u32[]{:S(2)}) copy-start(s32[2,8]{1,0:T(2,128)} %remote_ref.1) | copy-start | bytes 196
  0.7 149.7 %copy-start.5 = (f32[2,256]{1,0:T(2,128)S(1)}, f32[2,256]{1,0:T(2,128)}, u32[]{:S(2)}) copy-start(f32[2,256]{1,0:T(2,128)} %lse_ref.1) | copy-start | bytes 6148
  0.7 149.7 %copy-start.2 = (bf16[256,256]{1,0:T(8,128)(2,1)S(1)}, bf16[256,256]{1,0:T(8,128)(2,1)}, u32[]{:S(2)}) copy-start(bf16[256,256]{1,0:T(8,128)(2,1)} %g_ref.1) | copy-start | bytes 393220
  0.7 149.7 %copy-start.4 = (bf16[256,256]{1,0:T(8,128)(2,1)S(1)}, bf16[256,256]{1,0:T(8,128)(2,1)}, u32[]{:S(2)}) copy-start(bf16[256,256]{1,0:T(8,128)(2,1)} %o_ref.1) | copy-start | bytes 393220
  0.7 149.7 %copy-start.1 = (bf16[256,256]{1,0:T(8,128)(2,1)S(1)}, bf16[256,256]{1,0:T(8,128)(2,1)}, u32[]{:S(2)}) copy-start(bf16[256,256]{1,0:T(8,128)(2,1)} %v_ref.1) | copy-start | bytes 393220
  0.7 149.7 %copy-start = (bf16[256,256]{1,0:T(8,128)(2,1)S(1)}, bf16[256,256]{1,0:T(8,128)(2,1)}, u32[]{:S(2)}) copy-start(bf16[256,256]{1,0:T(8,128)(2,1)} %k_ref.1) | copy-start | bytes 393220
  0.7 149.7 %copy-start.3 = (bf16[256,256]{1,0:T(8,128)(2,1)S(1)}, bf16[256,256]{1,0:T(8,128)(2,1)}, u32[]{:S(2)}) copy-start(bf16[256,256]{1,0:T(8,128)(2,1)} %q_ref.1) | copy-start | bytes 393220

commit v3 on v1

v3 whole, which is shorter than its diff:
```python
import functools

import jax
import jax.numpy as jnp
from jax import lax
from jax.experimental import pallas as pl
from jax.experimental.pallas import tpu as pltpu
from jax.sharding import PartitionSpec as P

HD = 128
BLOCK = 128
NY = 4
GROUPS = ((4, 4, 4), (5, 5), (5, 5), (5, 5))
CAPS = tuple(sum(sizes) for sizes in GROUPS)
FIRST = tuple(sum(CAPS[:yy]) for yy in range(NY))
EMPTY = sum(CAPS)
DEAD = 1e30
LOG2E = 1.4426950408889634
F32 = jnp.float32
BF16 = jnp.bfloat16
I32 = jnp.int32


def with_halo(cells, sides, width):
    for axis, dim in sides:
        count = lax.axis_size(axis)
        ends = count - 1
        head = lax.slice_in_dim(cells, 0, width, axis=dim)
        tail = lax.slice_in_dim(cells, cells.shape[dim] - width, cells.shape[dim], axis=dim)
        cells = jnp.concatenate(
            [
                lax.ppermute(tail, axis, [(i, (i + 1) % count) for i in range(ends)]),
                cells,
                lax.ppermute(head, axis, [((i + 1) % count, i) for i in range(ends)]),
            ],
            axis=dim,
        )
    return cells


def block_pairs(queries, grads, stats, keys, values, valid, scale):
    scores = (
        jnp.einsum("pxhd,pyhd->phxy", queries, keys, preferred_element_type=jnp.float32) * scale
    )
    weights = jnp.exp(scores - stats[0][..., None]) * valid[:, None, None, None]
    probs = weights.astype(jnp.bfloat16)
    grad_values = jnp.einsum("phxy,pxhd->pyhd", probs, grads, preferred_element_type=jnp.float32)
    grad_probs = jnp.einsum("pxhd,pyhd->phxy", grads, values, preferred_element_type=jnp.float32)
    grad_scores = (weights * (grad_probs - stats[1][..., None])).astype(jnp.bfloat16)
    grad_queries = (
        jnp.einsum("phxy,pyhd->pxhd", grad_scores, keys, preferred_element_type=jnp.float32) * scale
    )
    grad_keys = (
        jnp.einsum("phxy,pxhd->pyhd", grad_scores, queries, preferred_element_type=jnp.float32)
        * scale
    )
    return (grad_queries, grad_keys, grad_values)


def spread_terms(terms):
    padded = jnp.pad(terms[0], ((0, 2), (0, 0), (0, 0), (0, 0)))
    padded = padded + jnp.pad(terms[1], ((1, 1), (0, 0), (0, 0), (0, 0)))
    return padded + jnp.pad(terms[2], ((2, 0), (0, 0), (0, 0), (0, 0)))


def remote_pairs(
    part_query, part_grad, part_stats, key_table, value_table, key_index, live_in, scale
):
    senders = part_query.shape[0]
    head_count = part_query.shape[2]
    groups = senders // 8

    def remote_group(items):
        one_q, one_g, one_s, one_k, one_l = items
        return block_pairs(
            one_q,
            one_g,
            one_s.transpose(1, 0, 2, 3),
            key_table[one_k],
            value_table[one_k],
            one_l,
            scale,
        )

    group_shape = (groups, 8, BLOCK, head_count, HD)
    found_q, found_k, found_v = lax.map(
        remote_group,
        (
            part_query.reshape(group_shape),
            part_grad.reshape(group_shape),
            part_stats.reshape(groups, 8, 2, head_count, BLOCK),
            key_index.reshape(groups, 8),
            live_in.reshape(groups, 8),
        ),
    )
    out_shape = (senders, BLOCK, head_count, HD)
    return (found_q.reshape(out_shape), found_k.reshape(out_shape), found_v.reshape(out_shape))


def general(query, key, value, output, grad_out, logsumexp, remote_blocks, remote_count):
    seq_size = lax.axis_size("seq")
    place = lax.axis_index("seq")
    rows, width = query.shape
    count_blocks = rows // BLOCK
    heads_here = width // HD
    scale = float(HD) ** (-0.5)
    shape_four = (count_blocks, BLOCK, heads_here, HD)
    q_tiles = query.reshape(shape_four)
    g_tiles = grad_out.reshape(shape_four)
    k_tiles = key.reshape(shape_four)
    v_tiles = value.reshape(shape_four)
    delta = jnp.sum(
        grad_out.astype(jnp.float32).reshape(shape_four)
        * output.astype(jnp.float32).reshape(shape_four),
        axis=3,
    )
    stats = jnp.stack(
        [
            logsumexp.reshape(heads_here, count_blocks, BLOCK).transpose(1, 0, 2),
            delta.transpose(0, 2, 1),
        ]
    )
    slots_used = (
        jnp.arange(remote_blocks.shape[1], dtype=jnp.int32)[None, :] < remote_count[:, None]
    )
    owners = remote_blocks // count_blocks
    local_key = remote_blocks % count_blocks
    match = (
        (owners[:, :, None] == jnp.arange(seq_size, dtype=jnp.int32)[None, None, :])
        & slots_used[:, :, None]
    ).astype(jnp.int32)
    live = jnp.sum(match, axis=(0, 1))
    send_query = jnp.sum(
        match * jnp.arange(count_blocks, dtype=jnp.int32)[:, None, None], axis=(0, 1)
    )
    send_key = jnp.sum(match * local_key[:, :, None], axis=(0, 1))
    meta = jnp.stack([send_key, live], axis=1).astype(jnp.float32)
    got_stats, got_meta = (
        lax.all_to_all(
            stats[:, send_query].transpose(1, 0, 2, 3),
            "seq",
            split_axis=0,
            concat_axis=0,
            tiled=True,
        ),
        lax.all_to_all(meta, "seq", split_axis=0, concat_axis=0, tiled=True),
    )
    key_index = got_meta[:, 0].astype(jnp.int32)
    live_in = got_meta[:, 1]
    got_query, got_grad = (
        lax.all_to_all(q_tiles[send_query], "seq", split_axis=0, concat_axis=0, tiled=True),
        lax.all_to_all(g_tiles[send_query], "seq", split_axis=0, concat_axis=0, tiled=True),
    )
    remote_q, remote_k, remote_v = remote_pairs(
        got_query, got_grad, got_stats, k_tiles, v_tiles, key_index, live_in, scale
    )
    returned = lax.all_to_all(
        remote_q.astype(jnp.bfloat16), "seq", split_axis=0, concat_axis=0, tiled=True
    )
    empty = jnp.zeros((count_blocks, BLOCK, width), jnp.float32)
    grad_key = empty.at[key_index].add(remote_k.reshape(seq_size, BLOCK, width))
    grad_value = empty.at[key_index].add(remote_v.reshape(seq_size, BLOCK, width))
    grad_query = empty.at[send_query].add(
        returned.reshape(seq_size, BLOCK, width).astype(jnp.float32)
    )
    offsets = jnp.arange(3, dtype=jnp.int32)[:, None]
    band_index = (
        place * count_blocks + jnp.arange(count_blocks, dtype=jnp.int32)[None, :] + offsets - 1
    )
    band_ok = (
        ((band_index >= 0) & (band_index < count_blocks * seq_size)).astype(jnp.float32).reshape(-1)
    )
    rimmed = with_halo(jnp.stack([key, value]), (("seq", 1),), BLOCK)
    wide = rimmed.reshape(2, count_blocks + 2, BLOCK, heads_here, HD)
    band_keys = jnp.concatenate([wide[0, j : j + count_blocks] for j in range(3)])
    band_values = jnp.concatenate([wide[1, j : j + count_blocks] for j in range(3)])
    band_q, band_k, band_v = block_pairs(
        jnp.concatenate([q_tiles] * 3),
        jnp.concatenate([g_tiles] * 3),
        jnp.concatenate([stats] * 3, axis=1),
        band_keys,
        band_values,
        band_ok,
        scale,
    )
    grad_query = grad_query + jnp.sum(band_q.reshape(3, count_blocks, BLOCK, width), axis=0)
    spread_k = spread_terms(band_k.reshape(3, count_blocks, BLOCK, heads_here, HD))
    spread_v = spread_terms(band_v.reshape(3, count_blocks, BLOCK, heads_here, HD))
    both = jnp.stack([spread_k, spread_v]).reshape(2, count_blocks + 2, BLOCK, width)
    edges = jnp.stack([both[:, 0], both[:, count_blocks + 1]])
    arrived = with_halo(edges, (("seq", 0),), 1)
    own = both[:, 1 : count_blocks + 1]
    own = own.at[:, 0].add(arrived[0]).at[:, count_blocks - 1].add(arrived[3])
    grad_key = grad_key + own[0]
    grad_value = grad_value + own[1]
    return (
        grad_query.reshape(rows, width).astype(jnp.bfloat16),
        grad_key.reshape(rows, width).astype(jnp.bfloat16),
        grad_value.reshape(rows, width).astype(jnp.bfloat16),
    )


def dot(a, b, ca, cb):
    return lax.dot_general(a, b, (((ca,), (cb,)), ((), ())), preferred_element_type=F32)


CUT = ()
FINE = (0, 1)
CHAINS = [(u, j) for u in range(6) for j in ((0, 1) if u in FINE else (2,))]


def last(u, j, d, half):
    if j < 2:
        return half if j == d else half - 1
    return half if u < 4 or d == 0 else half - 1


def plan(half, release=(1, 4, 0), lat=1.8, chunk=0.3, tab=4.0, bw=47.0, hop=0.3, iss=0.1):
    mid = half // 2
    steps = {}

    for u, j in CHAINS:
        cut = u > 3
        for d in range(2):
            for k in range(last(u, j, d, half) + 1):
                def size(n):
                    return 4 if u > 3 else 64 if n < half and j == 2 else 32
                sends = []
                if k < last(u, j, d, half) and not (cut and k == mid):
                    sends.append((("z", u, j, d, k + 1), d, size(k + 1), 1))
                if k == 0 and cut and mid < last(u, j, d, half):
                    sends.append((("z", u, j, d, mid + 1), d, size(mid + 1), mid + 1))
                needs = [("z", u, j, d, k - 1)] if k else []
                if k == 0 and 0 < u < 4:
                    pj = 0 if u - 1 in FINE else 2
                    needs = [("z", u - 1, pj, d, min(release[u - 1], half - 1))]
                awaits = [("z", u, j, d, k)] if k else []
                steps["z", u, j, d, k] = (needs, awaits, sends, 0.0)

    def all_in(u):
        return [("z", c, j, d, last(c, j, d, half)) for c, j in CHAINS if c == u for d in range(2)]

    for d in range(2):
        steps["ks", d] = ([("z", *CHAINS[0], 1, 0)], [], [(("k", d), 3 - d, 256, 1)], 0.1)
        steps["kw", d] = ([], [("k", d)], [(("k2", d), 3 - d, 128, 1)], 0.4)
    steps["kx",] = ([("kw", 0), ("kw", 1)], [("k2", 0), ("k2", 1)], [], 0.4)
    steps["tab",] = (all_in(5), [], [], tab)
    stats_in = all_in(4)
    for u in (4, 5):
        steps["zq", u] = ([("tab",)] + all_in(u), [], [], 0.5)
    for h in range(2):
        got = [all_in(2 * h + t) for t in range(2)]
        pairs = []
        for yy in (2, 1, 3, 0):
            keys = {0: [], 1: [("kw", 0)], 2: [("kx",)], 3: [("kw", 1)]}[yy]
            for i, size in enumerate(GROUPS[yy]):
                needs = [("tab",)] + stats_in + got[0] + got[1] + keys
                steps["own", h, yy, i] = (needs, [], [], size / 2 * chunk)
                pairs.append(("own", h, yy, i))
        far = [p for p in pairs if p[2] == 2]
        steps["d1", h] = (far, [], [(("d1", h, d), 2 + d, 68, 1) for d in range(2)], 0.2)
        sends = [(("d2", h, d), 2 + d, 132, 1) for d in range(2)]
        steps["d2", h] = (pairs + [("d1", h)], [("d1", h, d) for d in range(2)], sends, 0.3)
        steps["kv", h] = ([("d2", h)], [("d2", h, d) for d in range(2)], [], 0.3)
        fin = []
        for d in range(2):
            for j in range(2):
                for k in range(1, half + 1):
                    if k > 1 or j == d:
                        cut = h in CUT
                        first = k == 1 or (k == 2 and j != d) or (cut and k == mid + 1)
                        awaits = [] if first else [("s", h, d, j, k - 1)]
                        hops = mid + 1 if cut and k == mid else 1
                        if k == half or (cut and k == mid):
                            fin.append(("s", h, d, j, k))
                        steps["s", h, d, j, k] = (pairs + [("kv", 0)] * h, awaits, [(("s", h, d, j, k), 1 - d, 32, hops)], 0.12)
        for t in range(2):
            steps["zq", 2 * h + t] = (got[t] + pairs, [], [], 0.5)
        steps["yq", h] = ([("kv", h)], [], [], 0.5)
        steps["e", h] = (pairs, fin, [], 0.3)
    for s in list(steps):
        n, a, sd, c = steps[s]
        steps[s] = (n, a, sd, c + iss * (len(a) + len(sd)))
    sender = {m: (s, kib, hops) for s, (_, _, sends, _) in steps.items() for m, _, kib, hops in sends}
    after = {s: [] for s in steps}
    for s, (needs, awaits, _, _) in steps.items():
        for n in needs:
            after[n].append((s, 0.0))
        for m in awaits:
            f, kib, hops = sender[m]
            after[f].append((s, hops * kib / bw + lat + hop * (hops - 1)))
    way = {}

    def length(s):
        if s not in way:
            way[s] = steps[s][3] + max([gap + length(n) for n, gap in after[s]], default=0.0)
        return way[s]

    left = sorted(steps, key=lambda s: (-length(s), str(s)))
    now, free, arrival, done, order = 0.0, [0.0] * 4, {}, set(), []
    while left:
        ready = [
            (max([now] + [arrival[m] for m in steps[s][1]]), i)
            for i, s in enumerate(left)
            if all(n in done for n in steps[s][0]) and all(m in arrival for m in steps[s][1])
        ]
        now, i = min(ready)
        s = left.pop(i)
        now += steps[s][3]
        for m, link, kib, hops in steps[s][2]:
            begin = max(free[link], now)
            free[link] = begin + hops * kib / bw
            arrival[m] = begin + min(hops, 2) * kib / bw + lat + hop * (hops - 1)
        done.add(s)
        order.append(s)
    return order


def kernel(
    nz,
    remote_ref,
    count_ref,
    q_ref,
    k_ref,
    v_ref,
    o_ref,
    g_ref,
    lse_ref,
    dq_ref,
    dk_ref,
    dv_ref,
    over_ref,
    agq0,
    agq1,
    agg0,
    agg1,
    ags,
    meta,
    full,
    nkv,
    nkt,
    d1snd,
    d1rcv,
    dsnd,
    drcv,
    own0,
    own1,
    rsnd,
    rrcv,
    dkacc,
    dvacc,
    kt_ref,
    table,
    lists,
    nxt,
    pos,
    idx,
    msk,
    t_sem,
    z_send,
    z_recv,
    k_send,
    k_recv,
    k2_send,
    k2_recv,
    d1_send,
    d1_recv,
    d_send,
    d_recv,
    s_send,
    s_recv,
):
    me = lax.axis_index("seq")
    y = me // nz
    z = me % nz
    half = nz // 2
    cands = 2 * nz
    scale = float(HD) ** -0.5
    zdev = [y * nz + lax.rem(z + 1, nz), y * nz + lax.rem(z + nz - 1, nz)]
    ydev = [lax.rem(y + 1, NY) * nz + z, lax.rem(y + NY - 1, NY) * nz + z]
    mid = half // 2
    zfar = [y * nz + lax.rem(z + mid + 1, nz), y * nz + lax.rem(z + nz - mid - 1, nz)]
    agq = [agq0, agq1]
    agg = [agg0, agg1]
    own = [own0, own1]
    chain_refs = [agq0, agg0, agq1, agg1]

    barrier = pltpu.get_barrier_semaphore()
    for dev in zdev + zfar + ydev:
        pl.semaphore_signal(
            barrier, inc=1, device_id={"seq": dev}, device_id_type=pl.DeviceIdType.MESH
        )

    def put_blocks(ref, own_ref, h):
        for j in range(2):
            ref[2 * z + j] = own_ref[j * BLOCK : (j + 1) * BLOCK, h * HD : (h + 1) * HD]

    line = lax.broadcasted_iota(I32, (8, BLOCK), 0)
    lane = lax.broadcasted_iota(I32, (8, BLOCK), 1)

    def put_rows():
        rows = jnp.zeros((8, BLOCK), I32)
        for j in range(2):
            hit = jnp.where(jnp.abs(lane - (2 * me + j)) <= 1, 1, 0)
            for r in range(remote_ref.shape[1]):
                used = jnp.where(count_ref[j] > r, 1, 0)
                hit = jnp.maximum(hit, jnp.where(lane == remote_ref[j, r], used, 0))
            rows = jnp.where(line == j, hit, rows)
        meta[z] = rows

    def put_stats():
        for h in range(2):
            cols = slice(h * HD, (h + 1) * HD)
            for j in range(2):
                rows = slice(j * BLOCK, (j + 1) * BLOCK)
                prod = g_ref[rows, cols].astype(F32) * o_ref[rows, cols].astype(F32)
                at = 4 * h + 2 * j
                ags[z, at : at + 1, :] = lse_ref[h : h + 1, rows] * LOG2E
                ags[z, at + 1 : at + 2, :] = jnp.sum(prod.T, axis=0, keepdims=True)

    def put_rest():
        for h in range(2):
            own[h][EMPTY] = jnp.zeros((HD, BLOCK), F32)
            for n in range(NY):
                dkacc[h, n] = jnp.zeros((2 * BLOCK, HD), F32)
                dvacc[h, n] = jnp.zeros((2 * BLOCK, HD), F32)
            kt_ref[h] = k_ref[:, h * HD : (h + 1) * HD].T

    put_blocks(agq[0], q_ref, 0)
    put_rows()
    pl.semaphore_wait(barrier, 6)

    def remote(src, dst, send, recv, dev):
        return pltpu.make_async_remote_copy(
            src_ref=src,
            dst_ref=dst,
            send_sem=send,
            recv_sem=recv,
            device_id={"seq": dev},
            device_id_type=pl.DeviceIdType.MESH,
        )

    def z_view(u, j, d, k, at):
        if u > 3:
            return (ags, meta)[u - 4].at[at]
        if j == 2 and k < half:
            return chain_refs[u].at[pl.ds(2 * at, 2)]
        return chain_refs[u].at[pl.ds(2 * at + (d if j == 2 else j), 1)]

    def z_copy(u, j, d, k, receiving=False):
        direct = u > 3 and k == mid + 1
        hop = k if receiving else 0 if direct else k - 1
        at = lax.rem(z + nz - hop, nz) if d == 0 else lax.rem(z + hop, nz)
        view = z_view(u, j, d, k, at)
        c = CHAINS.index((u, j))
        sems = z_send.at[c, d, k - 1], z_recv.at[c, d, k - 1]
        return remote(view, view, *sems, (zfar if direct else zdev)[d])

    def z_step(u, j, d, k):
        if k > 0:
            z_copy(u, j, d, k, receiving=True).wait_recv()
        end = last(u, j, d, half)
        if k < end and not (u > 3 and k == mid):
            z_copy(u, j, d, k + 1).start()
        if k == 0 and u > 3 and mid < end:
            z_copy(u, j, d, mid + 1).start()

    def z_drain(u):
        for c, j in CHAINS:
            if c == u:
                for d in range(2):
                    for k in range(1, last(u, j, d, half) + 1):
                        z_copy(u, j, d, k).wait_send()

    def build_tables():
        copy = pltpu.make_async_copy(meta, table, t_sem)
        copy.start()
        copy.wait()

        def bit(c, yy, b):
            return table[c // 2, c % 2, lax.rem(y + yy, NY) * cands + 2 * z + b]

        def scan(c, carry):
            count = []
            for yy in range(NY):
                live = bit(c, yy, 0) | bit(c, yy, 1)
                place = jnp.where(carry[yy] < CAPS[yy], FIRST[yy] + carry[yy], EMPTY)
                pos[yy, c] = jnp.where(live > 0, place, EMPTY)
                lists[yy, c] = live
                count.append(carry[yy] + live)
            return tuple(count)

        counts = lax.fori_loop(0, cands, scan, (jnp.int32(0),) * NY)
        most = counts[0] - CAPS[0]
        for yy in range(1, NY):
            most = jnp.maximum(most, counts[yy] - CAPS[yy])
        full[...] = jnp.broadcast_to(jnp.where(most > 0, 1.0, 0.0).astype(F32), (8, BLOCK))

        for yy in range(NY):
            nxt[yy, cands] = jnp.int32(cands)
            nxt[yy, cands + 1] = jnp.int32(cands)

        def back(i, carry):
            c = cands - 1 - i
            out = []
            for yy in range(NY):
                cur = jnp.where(lists[yy, c] > 0, c, carry[yy])
                nxt[yy, c] = cur
                out.append(cur)
            return tuple(out)

        lax.fori_loop(0, cands, back, (jnp.int32(cands),) * NY)

        for yy in range(NY):
            cur = nxt[yy, 0]
            for p in range(FIRST[yy], FIRST[yy] + CAPS[yy]):
                c = jnp.minimum(cur, cands - 1)
                live = jnp.where(cur < cands, 1, 0)
                idx[p] = c
                msk[0, p] = live * bit(c, yy, 0)
                msk[1, p] = live * bit(c, yy, 1)
                cur = nxt[yy, jnp.minimum(cur + 1, cands + 1)]

    def pairs(h, n, queries, grads, lse0, lse1, delta):
        cols = slice(h * HD, (h + 1) * HD)
        keys = nkv[n - 1, 0, :, cols] if n else k_ref[:, cols]
        values = nkv[n - 1, 1, :, cols] if n else v_ref[:, cols]
        scores = dot(keys, queries, 1, 1) * (scale * LOG2E)
        weights = jnp.concatenate(
            [jnp.exp2(scores[:BLOCK] - lse0), jnp.exp2(scores[BLOCK:] - lse1)], axis=0
        )
        dvacc[h, n] += dot(weights.astype(BF16), grads, 1, 0)
        grad_probs = dot(values, grads, 1, 1)
        grad_scores = (weights * (grad_probs - delta)).astype(BF16)
        dkacc[h, n] += dot(grad_scores, queries, 1, 0)
        return dot(nkt[n - 1, h] if n else kt_ref[h], grad_scores, 1, 0) * scale

    def stat_rows(h, c):
        tile = ags[c // 2]
        odd = c % 2 > 0
        lse = jnp.where(odd, tile[4 * h + 2 : 4 * h + 3], tile[4 * h : 4 * h + 1])
        delta = jnp.where(odd, tile[4 * h + 3 : 4 * h + 4], tile[4 * h + 1 : 4 * h + 2])
        return lse, delta

    def join(parts, axis):
        return jnp.concatenate(parts, axis=axis)

    def list_pairs(h, yy, i):
        lo = FIRST[yy] + sum(GROUPS[yy][:i])
        hi = lo + GROUPS[yy][i]
        qs, gs, l0, l1, dl = [], [], [], [], []
        for p in range(lo, hi):
            c = idx[p]
            lse, delta = stat_rows(h, c)
            qs.append(agq[h][c])
            gs.append(agg[h][c])
            l0.append(jnp.where(msk[0, p] > 0, lse, DEAD))
            l1.append(jnp.where(msk[1, p] > 0, lse, DEAD))
            dl.append(delta)
        n = (0, 1, 3, 2)[yy]
        got = pairs(h, n, join(qs, 0), join(gs, 0), join(l0, 1), join(l1, 1), join(dl, 1))
        for p in range(lo, hi):
            own[h][p] = got[:, (p - lo) * BLOCK : (p - lo + 1) * BLOCK]

    def k_copy(d, n):
        src = (k_ref, v_ref)[n]
        return remote(src, nkv.at[d, n], k_send.at[d, n], k_recv.at[d, n], ydev[1 - d])

    def keys_send(d):
        for n in range(2):
            k_copy(d, n).start()

    def k2_copy(d):
        src, dst = nkv.at[d, d], nkv.at[2, d]
        return remote(src, dst, k2_send.at[d], k2_recv.at[d], ydev[1 - d])

    def keys_wait(d):
        for n in range(2):
            k_copy(d, n).wait_recv()
        k2_copy(d).start()
        for h in range(2):
            nkt[d, h] = nkv[d, 0, :, h * HD : (h + 1) * HD].T

    def keys_end():
        for d in range(2):
            k2_copy(d).wait_recv()
        for h in range(2):
            nkt[2, h] = nkv[2, 0, :, h * HD : (h + 1) * HD].T

    def d1_copy(h, d):
        sems = d1_send.at[h, d], d1_recv.at[h, d]
        return remote(d1snd.at[h, d], d1rcv.at[h, d], *sems, ydev[d])

    def d_copy(h, d):
        return remote(dsnd.at[h, d], drcv.at[h, d], d_send.at[h, d], d_recv.at[h, d], ydev[d])

    def far_send(h):
        for d in range(2):
            d1snd[h, d, : 2 * BLOCK] = (dkacc, dvacc)[d][h, 3].astype(BF16)
            d1snd[h, d, 2 * BLOCK :] = jnp.broadcast_to(full[0:1], (16, HD)).astype(BF16)
            d1_copy(h, d).start()

    def near_send(h):
        seen = full[0:1]
        for d in range(2):
            d1_copy(h, d).wait_recv()
            seen = jnp.maximum(seen, d1rcv[h, d, 2 * BLOCK :].astype(F32)[0:1])
        for d in range(2):
            sums = [dkacc[h, 1 + d], dvacc[h, 1 + d]]
            sums[d] = sums[d] + d1rcv[h, d, : 2 * BLOCK].astype(F32)
            dsnd[h, d, 0 : 2 * BLOCK] = sums[0].astype(BF16)
            dsnd[h, d, 2 * BLOCK : 4 * BLOCK] = sums[1].astype(BF16)
            dsnd[h, d, 4 * BLOCK :] = jnp.broadcast_to(seen, (16, HD)).astype(BF16)
            d_copy(h, d).start()

    def terms(h, at, j):
        c = 2 * at + j
        total = own[h][pos[0, c]]
        for yy in range(1, NY):
            total = total + own[h][pos[yy, c]]
        return total

    def s_copy(h, d, j, k):
        at = pl.ds(0, BLOCK + 16 if h == 1 and j == d else BLOCK)
        return remote(
            rsnd.at[h, d, j, k - 1, at],
            rrcv.at[h, d, j, k - 1, at],
            s_send.at[h, d, j, k - 1],
            s_recv.at[h, d, j, k - 1],
            (zfar if h in CUT and k == mid else zdev)[1 - d],
        )

    extra = slice(BLOCK, BLOCK + 16)

    def s_step(h, d, j, k):
        dist = half + 1 - k
        at = lax.rem(z + nz - dist, nz) if d == 0 else lax.rem(z + dist, nz)
        total = terms(h, at, j)
        carries = h == 1 and j == d
        if carries:
            rsnd[h, d, j, k - 1, extra] = jnp.broadcast_to(full[0:1], (16, HD)).astype(BF16)
        cut = h in CUT
        if (k > 2 or (k == 2 and j == d)) and not (cut and k == mid + 1):
            s_copy(h, d, j, k - 1).wait_recv()
            total = total + rrcv[h, d, j, k - 2, :BLOCK].astype(F32)
            if carries:
                rsnd[h, d, j, k - 1, extra] = jnp.maximum(
                    rsnd[h, d, j, k - 1, extra], rrcv[h, d, j, k - 2, extra]
                )
        rsnd[h, d, j, k - 1, :BLOCK] = total.astype(BF16)
        s_copy(h, d, j, k).start()
        if k - 2 >= (mid + 1 if cut and k > mid else 1 if j == d else 2):
            s_copy(h, d, j, k - 2).wait_send()

    def s_end(h):
        cols = slice(h * HD, (h + 1) * HD)
        any_full = full[0:1]
        for j in range(2):
            total = terms(h, z, j)
            for d in range(2):
                for k in (mid, half) if h in CUT else (half,):
                    if k > 1 or j == d:
                        s_copy(h, d, j, k).wait_recv()
                        total = total + rrcv[h, d, j, k - 1, :BLOCK].astype(F32)
                        if h == 1 and j == d:
                            got = rrcv[h, d, j, k - 1, extra].astype(F32)
                            any_full = jnp.maximum(any_full, got[0:1])
                lo = 1 if j == d else 2
                for lo, hi in ((lo, mid), (mid + 1, half)) if h in CUT else ((lo, half),):
                    for k in range(max(lo, hi - 1), hi + 1):
                        s_copy(h, d, j, k).wait_send()
            dq_ref[j * BLOCK : (j + 1) * BLOCK, cols] = total.T.astype(BF16)
        if h == 1:
            over_ref[...] = jnp.broadcast_to(any_full, (8, BLOCK))

    def results(h):
        cols = slice(h * HD, (h + 1) * HD)
        grad_k, grad_v = dkacc[h, 0], dvacc[h, 0]
        seen = full[0:1]
        for d in range(2):
            d_copy(h, d).wait_recv()
            grad_k = grad_k + drcv[h, d, 0 : 2 * BLOCK].astype(F32)
            grad_v = grad_v + drcv[h, d, 2 * BLOCK : 4 * BLOCK].astype(F32)
            seen = jnp.maximum(seen, drcv[h, d, 4 * BLOCK :].astype(F32)[0:1])
        dk_ref[:, cols] = (grad_k * scale).astype(BF16)
        dv_ref[:, cols] = grad_v.astype(BF16)
        if h == 0:
            full[...] = jnp.broadcast_to(seen, (8, BLOCK))

    def y_drain(h):
        k2_copy(h).wait_send()
        for d in range(2):
            k_copy(d, h).wait_send()
            d1_copy(h, d).wait_send()
            d_copy(h, d).wait_send()

    do = {
        "z": z_step,
        "tab": build_tables,
        "own": list_pairs,
        "ks": keys_send,
        "kw": keys_wait,
        "kx": keys_end,
        "d1": far_send,
        "d2": near_send,
        "kv": results,
        "zq": z_drain,
        "yq": y_drain,
        "s": s_step,
        "e": s_end,
    }
    steps = plan(half)
    ahead = [("z", *c, d, 0) for c in CHAINS if c[0] == 0 for d in range(2)]
    ahead += [("ks", 0), ("ks", 1)]
    for step in ahead:
        do[step[0]](*step[1:])
    put_stats()
    for u in range(1, 4):
        put_blocks(chain_refs[u], (q_ref, g_ref)[u % 2], u // 2)
    put_rest()
    for step in steps:
        if step not in ahead:
            do[step[0]](*step[1:])


def fast(nz, remote, count, query, key, value, output, grad_out, logsumexp):
    rows, width = query.shape
    half = nz // 2
    blocks = (2 * nz, BLOCK, HD)
    vmem, dma = pltpu.VMEM, pltpu.SemaphoreType.DMA
    smem = pltpu.SMEM
    outs = [jax.ShapeDtypeStruct((rows, width), BF16)] * 3
    outs.append(jax.ShapeDtypeStruct((8, BLOCK), F32))
    in_vmem = pl.BlockSpec(memory_space=pltpu.VMEM)
    scratch = [
        *[vmem(blocks, BF16)] * 4,
        vmem((nz, 8, BLOCK), F32),
        vmem((nz, 8, BLOCK), I32),
        vmem((8, BLOCK), F32),
        vmem((3, 2, rows, width), BF16),
        vmem((3, 2, HD, 2 * BLOCK), BF16),
        vmem((2, 2, 2 * BLOCK + 16, HD), BF16),
        vmem((2, 2, 2 * BLOCK + 16, HD), BF16),
        vmem((2, 2, 4 * BLOCK + 16, HD), BF16),
        vmem((2, 2, 4 * BLOCK + 16, HD), BF16),
        *[vmem((EMPTY + 1, HD, BLOCK), F32)] * 2,
        vmem((2, 2, 2, half, BLOCK + 16, HD), BF16),
        vmem((2, 2, 2, half, BLOCK + 16, HD), BF16),
        vmem((2, NY, 2 * BLOCK, HD), F32),
        vmem((2, NY, 2 * BLOCK, HD), F32),
        vmem((2, HD, 2 * BLOCK), BF16),
        smem((nz, 8, BLOCK), I32),
        smem((NY, 2 * nz), I32),
        smem((NY, 2 * nz + 2), I32),
        smem((NY, 2 * nz), I32),
        smem((EMPTY,), I32),
        smem((2, EMPTY), I32),
        pltpu.SemaphoreType.DMA,
        *[dma((len(CHAINS), 2, half))] * 2,
        *[dma((2, 2))] * 2,
        *[dma((2,))] * 2,
        *[dma((2, 2))] * 2,
        *[dma((2, 2))] * 2,
        *[dma((2, 2, 2, half))] * 2,
    ]
    return pl.pallas_call(
        functools.partial(kernel, nz),
        out_shape=outs,
        in_specs=[pl.BlockSpec(memory_space=pltpu.SMEM)] * 2 + [in_vmem] * 6,
        out_specs=[in_vmem] * 4,
        scratch_shapes=scratch,
        compiler_params=pltpu.CompilerParams(
            collective_id=0, has_side_effects=True, vmem_limit_bytes=48 * 1024 * 1024
        ),
        cost_estimate=pl.CostEstimate(
            flops=4 * 10**9, bytes_accessed=4 * 2**20, transcendentals=5 * 10**6
        ),
    )(remote, count, query, key, value, output, grad_out, logsumexp)


def per_device(query, key, value, output, grad_out, logsumexp, remote_blocks, remote_count):
    nz = lax.axis_size("seq") // NY
    *found, over = fast(
        nz, remote_blocks, remote_count, query, key, value, output, grad_out, logsumexp
    )
    return lax.cond(
        over[0, 0] > 0,
        lambda: general(
            query, key, value, output, grad_out, logsumexp, remote_blocks, remote_count
        ),
        lambda: tuple(found),
    )


def solution(mesh):
    return jax.shard_map(
        per_device,
        mesh=mesh,
        in_specs=(
            P("seq", "head"),
            P("seq", "head"),
            P("seq", "head"),
            P("seq", "head"),
            P("seq", "head"),
            P("head", "seq"),
            P("seq", None),
            P("seq"),
        ),
        out_specs=(P("seq", "head"), P("seq", "head"), P("seq", "head")),
        check_vma=False,
    )
```

time: 139 us -> 110 us (0.79)
  the two profiles are of different devices: /device:TPU:2 before, /device:TPU:24 now
where the time goes in v3:
time: 110 us
  Pallas kernels  105 us (95%)
  local copies, waits for them, and re-layouts  2.51 us (2%)
  between operations  1.43 us (1%)
    pallas_call x1, Pallas kernels, fast(): pl.pallas_call(functools.partial(kernel, nz), out_shape=outs, in_specs=[p...  105 us

profile of v3, /device:TPU:24, one launch (start us, length us, event | category | flops | bytes accessed | tf_op | source)
XLA Modules:
  0.0 109.6 jit_solution(7740012023586360972)
XLA Ops:
  0.6 0.0 copy-start.8
  0.6 0.0 copy-start.6
  0.7 0.0 copy-start.5
  0.7 0.0 copy-start.2
  0.7 0.0 copy-start.4
  0.7 0.0 copy-start.1
  0.7 0.0 copy-start
  0.7 0.0 copy-start.3
  0.7 105.4 %shard_map.109 = (bf16[256,256]{1,0:T(8,128)(2,1)S(1)}, bf16[256,256]{1,0:T(8,128)(2,1)S(1)}, bf16[256,256]{1,0:T(8,128)(2,1)S(1)}, f32[8,128]{1,0:T(8,128)S(1)}) custom-call(s32[2,8]{1,0:T(2,128)} %remote_ref.1, s32[2]{0:T(128)} %count_ref.1, bf16[256,256]{1,0:T(8,128)(2,1)} %q_ref.1, bf16[256,256]{1,0:T(8,128)(2,1)} %k_ref.1, bf16[256,256]{1,0:T(8,128)(2,1)} %v_ref.1, ...), custom_call_target="tpu_custom_call" | custom-call | flops 4000000000 | bytes 4194304 | tf_op jit(solution)/shard_map/pallas_call | solution.py:766
  106.2 0.5 slice.141
  107.3 0.0 copy-done.8
  107.3 0.0 copy-done.6
  107.3 0.0 copy-done.5
  107.3 0.0 copy-done.2
  107.4 0.0 copy-done.4
  107.4 0.0 copy-done.1
  107.4 0.0 copy-done
  107.4 0.0 copy-done.3
  107.4 0.3 conditional.1
  107.7 0.7 copy.284
  108.3 0.7 copy.285
  109.0 0.7 copy.286
Async XLA Ops:
  0.6 106.7 %copy-start.8 = (s32[2]{0:T(128)S(1)}, s32[2]{0:T(128)}, u32[]{:S(2)}) copy-start(s32[2]{0:T(128)} %count_ref.1) | copy-start | bytes 28
  0.6 106.7 %copy-start.6 = (s32[2,8]{1,0:T(2,128)S(1)}, s32[2,8]{1,0:T(2,128)}, u32[]{:S(2)}) copy-start(s32[2,8]{1,0:T(2,128)} %remote_ref.1) | copy-start | bytes 196
  0.7 106.7 %copy-start.5 = (f32[2,256]{1,0:T(2,128)S(1)}, f32[2,256]{1,0:T(2,128)}, u32[]{:S(2)}) copy-start(f32[2,256]{1,0:T(2,128)} %lse_ref.1) | copy-start | bytes 6148
  0.7 106.7 %copy-start.2 = (bf16[256,256]{1,0:T(8,128)(2,1)S(1)}, bf16[256,256]{1,0:T(8,128)(2,1)}, u32[]{:S(2)}) copy-start(bf16[256,256]{1,0:T(8,128)(2,1)} %g_ref.1) | copy-start | bytes 393220
  0.7 106.7 %copy-start.4 = (bf16[256,256]{1,0:T(8,128)(2,1)S(1)}, bf16[256,256]{1,0:T(8,128)(2,1)}, u32[]{:S(2)}) copy-start(bf16[256,256]{1,0:T(8,128)(2,1)} %o_ref.1) | copy-start | bytes 393220
  0.7 106.7 %copy-start.1 = (bf16[256,256]{1,0:T(8,128)(2,1)S(1)}, bf16[256,256]{1,0:T(8,128)(2,1)}, u32[]{:S(2)}) copy-start(bf16[256,256]{1,0:T(8,128)(2,1)} %v_ref.1) | copy-start | bytes 393220
  0.7 106.7 %copy-start = (bf16[256,256]{1,0:T(8,128)(2,1)S(1)}, bf16[256,256]{1,0:T(8,128)(2,1)}, u32[]{:S(2)}) copy-start(bf16[256,256]{1,0:T(8,128)(2,1)} %k_ref.1) | copy-start | bytes 393220
  0.7 106.7 %copy-start.3 = (bf16[256,256]{1,0:T(8,128)(2,1)S(1)}, bf16[256,256]{1,0:T(8,128)(2,1)}, u32[]{:S(2)}) copy-start(bf16[256,256]{1,0:T(8,128)(2,1)} %q_ref.1) | copy-start | bytes 393220

commit v4 on v3

--- a/solution.py
+++ b/solution.py
@@ -10,7 +10,7 @@
 HD = 128
 BLOCK = 128
 NY = 4
-GROUPS = ((4, 4, 4), (5, 5), (5, 5), (5, 5))
+GROUPS = ((6, 6), (10,), (10,), (10,))
 CAPS = tuple(sum(sizes) for sizes in GROUPS)
 FIRST = tuple(sum(CAPS[:yy]) for yy in range(NY))
 EMPTY = sum(CAPS)
@@ -215,7 +215,7 @@
     return half if u < 4 or d == 0 else half - 1
 
 
-def plan(half, release=(1, 4, 0), lat=1.8, chunk=0.3, tab=4.0, bw=47.0, hop=0.3, iss=0.1):
+def plan(half, release=(1, 2, 0), lat=1.8, chunk=0.2, tab=4.0, bw=47.0, hop=0.3, iss=0.1):
     mid = half // 2
     steps = {}
 
@@ -247,7 +247,7 @@
     steps["tab",] = (all_in(5), [], [], tab)
     stats_in = all_in(4)
     for u in (4, 5):
-        steps["zq", u] = ([("tab",)] + all_in(u), [], [], 0.5)
+        steps["zq", u] = ([("tab",)] + all_in(u), [], [], 0.1)
     for h in range(2):
         got = [all_in(2 * h + t) for t in range(2)]
         pairs = []
@@ -273,10 +273,10 @@
                         hops = mid + 1 if cut and k == mid else 1
                         if k == half or (cut and k == mid):
                             fin.append(("s", h, d, j, k))
-                        steps["s", h, d, j, k] = (pairs + [("kv", 0)] * h, awaits, [(("s", h, d, j, k), 1 - d, 32, hops)], 0.12)
+                        steps["s", h, d, j, k] = (pairs + [("kv", 0)] * h, awaits, [(("s", h, d, j, k), 1 - d, 32, hops)], 0.08)
         for t in range(2):
-            steps["zq", 2 * h + t] = (got[t] + pairs, [], [], 0.5)
-        steps["yq", h] = ([("kv", h)], [], [], 0.5)
+            steps["zq", 2 * h + t] = (got[t] + pairs, [], [], 0.1)
+        steps["yq", h] = ([("kv", h)], [], [], 0.1)
         steps["e", h] = (pairs, fin, [], 0.3)
     for s in list(steps):
         n, a, sd, c = steps[s]
@@ -711,12 +711,12 @@
     }
     steps = plan(half)
     ahead = [("z", *c, d, 0) for c in CHAINS if c[0] == 0 for d in range(2)]
-    ahead += [("ks", 0), ("ks", 1)]
+    ahead += [("z", 5, 2, d, 0) for d in range(2)] + [("ks", 0), ("ks", 1)]
     for step in ahead:
         do[step[0]](*step[1:])
-    put_stats()
     for u in range(1, 4):
         put_blocks(chain_refs[u], (q_ref, g_ref)[u % 2], u // 2)
+    put_stats()
     put_rest()
     for step in steps:
         if step not in ahead:

time: 110 us -> 107 us (0.973)
  Pallas kernels: 105 us -> 103 us
    pallas_call x1, Pallas kernels: 105 us -> 103 us  [fast(): pl.pallas_call(functools.partial(kernel, nz), out_shape=outs, in_specs=[p...]
where the time goes in v4:
time: 107 us
  Pallas kernels  103 us (96%)
  local copies, waits for them, and re-layouts  2.51 us (2%)
  between operations  1.43 us (1%)
    pallas_call x1, Pallas kernels, fast(): pl.pallas_call(functools.partial(kernel, nz), out_shape=outs, in_specs=[p...  103 us

profile of v4, /device:TPU:24, one launch (start us, length us, event | category | flops | bytes accessed | tf_op | source)
XLA Modules:
  0.0 107.0 jit_solution(244246373405604725)
XLA Ops:
  0.6 0.0 copy-start.8
  0.6 0.0 copy-start.6
  0.7 0.0 copy-start.5
  0.7 0.0 copy-start.2
  0.7 0.0 copy-start.4
  0.7 0.0 copy-start.1
  0.7 0.0 copy-start
  0.7 0.0 copy-start.3
  0.7 102.8 %shard_map.109 = (bf16[256,256]{1,0:T(8,128)(2,1)S(1)}, bf16[256,256]{1,0:T(8,128)(2,1)S(1)}, bf16[256,256]{1,0:T(8,128)(2,1)S(1)}, f32[8,128]{1,0:T(8,128)S(1)}) custom-call(s32[2,8]{1,0:T(2,128)} %remote_ref.1, s32[2]{0:T(128)} %count_ref.1, bf16[256,256]{1,0:T(8,128)(2,1)} %q_ref.1, bf16[256,256]{1,0:T(8,128)(2,1)} %k_ref.1, bf16[256,256]{1,0:T(8,128)(2,1)} %v_ref.1, ...), custom_call_target="tpu_custom_call" | custom-call | flops 4000000000 | bytes 4194304 | tf_op jit(solution)/shard_map/pallas_call | solution.py:766
  103.6 0.5 slice.141
  104.7 0.0 copy-done.8
  104.7 0.0 copy-done.6
  104.7 0.0 copy-done.5
  104.8 0.0 copy-done.2
  104.8 0.0 copy-done.4
  104.8 0.0 copy-done.1
  104.8 0.0 copy-done
  104.8 0.0 copy-done.3
  104.8 0.2 conditional.1
  105.0 0.7 copy.284
  105.7 0.7 copy.285
  106.3 0.7 copy.286
Async XLA Ops:
  0.6 104.1 %copy-start.8 = (s32[2]{0:T(128)S(1)}, s32[2]{0:T(128)}, u32[]{:S(2)}) copy-start(s32[2]{0:T(128)} %count_ref.1) | copy-start | bytes 28
  0.6 104.1 %copy-start.6 = (s32[2,8]{1,0:T(2,128)S(1)}, s32[2,8]{1,0:T(2,128)}, u32[]{:S(2)}) copy-start(s32[2,8]{1,0:T(2,128)} %remote_ref.1) | copy-start | bytes 196
  0.7 104.1 %copy-start.5 = (f32[2,256]{1,0:T(2,128)S(1)}, f32[2,256]{1,0:T(2,128)}, u32[]{:S(2)}) copy-start(f32[2,256]{1,0:T(2,128)} %lse_ref.1) | copy-start | bytes 6148
  0.7 104.1 %copy-start.2 = (bf16[256,256]{1,0:T(8,128)(2,1)S(1)}, bf16[256,256]{1,0:T(8,128)(2,1)}, u32[]{:S(2)}) copy-start(bf16[256,256]{1,0:T(8,128)(2,1)} %g_ref.1) | copy-start | bytes 393220
  0.7 104.1 %copy-start.4 = (bf16[256,256]{1,0:T(8,128)(2,1)S(1)}, bf16[256,256]{1,0:T(8,128)(2,1)}, u32[]{:S(2)}) copy-start(bf16[256,256]{1,0:T(8,128)(2,1)} %o_ref.1) | copy-start | bytes 393220
  0.7 104.1 %copy-start.1 = (bf16[256,256]{1,0:T(8,128)(2,1)S(1)}, bf16[256,256]{1,0:T(8,128)(2,1)}, u32[]{:S(2)}) copy-start(bf16[256,256]{1,0:T(8,128)(2,1)} %v_ref.1) | copy-start | bytes 393220
  0.7 104.1 %copy-start = (bf16[256,256]{1,0:T(8,128)(2,1)S(1)}, bf16[256,256]{1,0:T(8,128)(2,1)}, u32[]{:S(2)}) copy-start(bf16[256,256]{1,0:T(8,128)(2,1)} %k_ref.1) | copy-start | bytes 393220
  0.7 104.1 %copy-start.3 = (bf16[256,256]{1,0:T(8,128)(2,1)S(1)}, bf16[256,256]{1,0:T(8,128)(2,1)}, u32[]{:S(2)}) copy-start(bf16[256,256]{1,0:T(8,128)(2,1)} %q_ref.1) | copy-start | bytes 393220

commit v5 on v4

--- a/solution.py
+++ b/solution.py
@@ -215,7 +215,7 @@
     return half if u < 4 or d == 0 else half - 1
 
 
-def plan(half, release=(1, 2, 0), lat=1.8, chunk=0.2, tab=4.0, bw=47.0, hop=0.3, iss=0.1):
+def plan(half, release=(0, 1, 0), lat=1.8, chunk=0.2, tab=3.0, bw=47.0, hop=0.3, iss=0.1):
     mid = half // 2
     steps = {}
 
@@ -231,9 +231,11 @@
                 if k == 0 and cut and mid < last(u, j, d, half):
                     sends.append((("z", u, j, d, mid + 1), d, size(mid + 1), mid + 1))
                 needs = [("z", u, j, d, k - 1)] if k else []
+                if k == 0 and u not in (0, 5):
+                    needs = [("put", u)]
                 if k == 0 and 0 < u < 4:
                     pj = 0 if u - 1 in FINE else 2
-                    needs = [("z", u - 1, pj, d, min(release[u - 1], half - 1))]
+                    needs += [("z", u - 1, pj, d, min(release[u - 1], half - 1))]
                 awaits = [("z", u, j, d, k)] if k else []
                 steps["z", u, j, d, k] = (needs, awaits, sends, 0.0)
 
@@ -244,7 +246,10 @@
         steps["ks", d] = ([("z", *CHAINS[0], 1, 0)], [], [(("k", d), 3 - d, 256, 1)], 0.1)
         steps["kw", d] = ([], [("k", d)], [(("k2", d), 3 - d, 128, 1)], 0.4)
     steps["kx",] = ([("kw", 0), ("kw", 1)], [("k2", 0), ("k2", 1)], [], 0.4)
-    steps["tab",] = (all_in(5), [], [], tab)
+    for u, cost in ((1, 0.2), (2, 0.2), (3, 0.2), (4, 1.2), (6, 1.5)):
+        steps["put", u] = ([], [], [], cost)
+    steps["tc",] = (all_in(5), [], [(("tc",), 4, 1, 1)], 0.1)
+    steps["tab",] = ([("tc",)], [("tc",)], [], tab)
     stats_in = all_in(4)
     for u in (4, 5):
         steps["zq", u] = ([("tab",)] + all_in(u), [], [], 0.1)
@@ -254,7 +259,7 @@
         for yy in (2, 1, 3, 0):
             keys = {0: [], 1: [("kw", 0)], 2: [("kx",)], 3: [("kw", 1)]}[yy]
             for i, size in enumerate(GROUPS[yy]):
-                needs = [("tab",)] + stats_in + got[0] + got[1] + keys
+                needs = [("tab",), ("put", 6)] + stats_in + got[0] + got[1] + keys
                 steps["own", h, yy, i] = (needs, [], [], size / 2 * chunk)
                 pairs.append(("own", h, yy, i))
         far = [p for p in pairs if p[2] == 2]
@@ -297,7 +302,7 @@
         return way[s]
 
     left = sorted(steps, key=lambda s: (-length(s), str(s)))
-    now, free, arrival, done, order = 0.0, [0.0] * 4, {}, set(), []
+    now, free, arrival, done, order = 0.0, [0.0] * 5, {}, set(), []
     while left:
         ready = [
             (max([now] + [arrival[m] for m in steps[s][1]]), i)
@@ -472,10 +477,14 @@
                     for k in range(1, last(u, j, d, half) + 1):
                         z_copy(u, j, d, k).wait_send()
 
+    def table_copy():
+        return pltpu.make_async_copy(meta, table, t_sem)
+
+    def table_start():
+        table_copy().start()
+
     def build_tables():
-        copy = pltpu.make_async_copy(meta, table, t_sem)
-        copy.start()
-        copy.wait()
+        table_copy().wait()
 
         def bit(c, yy, b):
             return table[c // 2, c % 2, lax.rem(y + yy, NY) * cands + 2 * z + b]
@@ -694,8 +703,18 @@
             d1_copy(h, d).wait_send()
             d_copy(h, d).wait_send()
 
+    def put(u):
+        if u == 4:
+            put_stats()
+        elif u == 6:
+            put_rest()
+        else:
+            put_blocks(chain_refs[u], (q_ref, g_ref)[u % 2], u // 2)
+
     do = {
         "z": z_step,
+        "put": put,
+        "tc": table_start,
         "tab": build_tables,
         "own": list_pairs,
         "ks": keys_send,
@@ -714,10 +733,6 @@
     ahead += [("z", 5, 2, d, 0) for d in range(2)] + [("ks", 0), ("ks", 1)]
     for step in ahead:
         do[step[0]](*step[1:])
-    for u in range(1, 4):
-        put_blocks(chain_refs[u], (q_ref, g_ref)[u % 2], u // 2)
-    put_stats()
-    put_rest()
     for step in steps:
         if step not in ahead:
             do[step[0]](*step[1:])

time: 107 us -> 106 us (level)
  the two profiles are of different devices: /device:TPU:24 before, /device:TPU:2 now
where the time goes in v5:
time: 106 us
  Pallas kernels  102 us (96%)
  local copies, waits for them, and re-layouts  2.51 us (2%)
  between operations  1.43 us (1%)
    pallas_call x1, Pallas kernels, fast(): pl.pallas_call(functools.partial(kernel, nz), out_shape=outs, in_specs=[p...  102 us

profile of v5, /device:TPU:2, one launch (start us, length us, event | category | flops | bytes accessed | tf_op | source)
XLA Modules:
  0.0 105.9 jit_solution(2322020638094491311)
XLA Ops:
  0.6 0.0 copy-start.8
  0.6 0.0 copy-start.6
  0.7 0.0 copy-start.5
  0.7 0.0 copy-start.2
  0.7 0.0 copy-start.4
  0.7 0.0 copy-start.1
  0.7 0.0 copy-start
  0.7 0.0 copy-start.3
  0.7 101.8 %shard_map.109 = (bf16[256,256]{1,0:T(8,128)(2,1)S(1)}, bf16[256,256]{1,0:T(8,128)(2,1)S(1)}, bf16[256,256]{1,0:T(8,128)(2,1)S(1)}, f32[8,128]{1,0:T(8,128)S(1)}) custom-call(s32[2,8]{1,0:T(2,128)} %remote_ref.1, s32[2]{0:T(128)} %count_ref.1, bf16[256,256]{1,0:T(8,128)(2,1)} %q_ref.1, bf16[256,256]{1,0:T(8,128)(2,1)} %k_ref.1, bf16[256,256]{1,0:T(8,128)(2,1)} %v_ref.1, ...), custom_call_target="tpu_custom_call" | custom-call | flops 4000000000 | bytes 4194304 | tf_op jit(solution)/shard_map/pallas_call | solution.py:781
  102.5 0.5 slice.141
  103.6 0.0 copy-done.8
  103.7 0.0 copy-done.6
  103.7 0.0 copy-done.5
  103.7 0.0 copy-done.2
  103.7 0.0 copy-done.4
  103.7 0.0 copy-done.1
  103.7 0.0 copy-done
  103.7 0.0 copy-done.3
  103.7 0.2 conditional.1
  104.0 0.7 copy.284
  104.6 0.7 copy.285
  105.3 0.7 copy.286
Async XLA Ops:
  0.6 103.0 %copy-start.8 = (s32[2]{0:T(128)S(1)}, s32[2]{0:T(128)}, u32[]{:S(2)}) copy-start(s32[2]{0:T(128)} %count_ref.1) | copy-start | bytes 28
  0.6 103.0 %copy-start.6 = (s32[2,8]{1,0:T(2,128)S(1)}, s32[2,8]{1,0:T(2,128)}, u32[]{:S(2)}) copy-start(s32[2,8]{1,0:T(2,128)} %remote_ref.1) | copy-start | bytes 196
  0.7 103.0 %copy-start.5 = (f32[2,256]{1,0:T(2,128)S(1)}, f32[2,256]{1,0:T(2,128)}, u32[]{:S(2)}) copy-start(f32[2,256]{1,0:T(2,128)} %lse_ref.1) | copy-start | bytes 6148
  0.7 103.0 %copy-start.2 = (bf16[256,256]{1,0:T(8,128)(2,1)S(1)}, bf16[256,256]{1,0:T(8,128)(2,1)}, u32[]{:S(2)}) copy-start(bf16[256,256]{1,0:T(8,128)(2,1)} %g_ref.1) | copy-start | bytes 393220
  0.7 103.0 %copy-start.4 = (bf16[256,256]{1,0:T(8,128)(2,1)S(1)}, bf16[256,256]{1,0:T(8,128)(2,1)}, u32[]{:S(2)}) copy-start(bf16[256,256]{1,0:T(8,128)(2,1)} %o_ref.1) | copy-start | bytes 393220
  0.7 103.0 %copy-start.1 = (bf16[256,256]{1,0:T(8,128)(2,1)S(1)}, bf16[256,256]{1,0:T(8,128)(2,1)}, u32[]{:S(2)}) copy-start(bf16[256,256]{1,0:T(8,128)(2,1)} %v_ref.1) | copy-start | bytes 393220
  0.7 103.0 %copy-start = (bf16[256,256]{1,0:T(8,128)(2,1)S(1)}, bf16[256,256]{1,0:T(8,128)(2,1)}, u32[]{:S(2)}) copy-start(bf16[256,256]{1,0:T(8,128)(2,1)} %k_ref.1) | copy-start | bytes 393220
  0.7 103.0 %copy-start.3 = (bf16[256,256]{1,0:T(8,128)(2,1)S(1)}, bf16[256,256]{1,0:T(8,128)(2,1)}, u32[]{:S(2)}) copy-start(bf16[256,256]{1,0:T(8,128)(2,1)} %q_ref.1) | copy-start | bytes 393220

commit v6 on v5

--- a/solution.py
+++ b/solution.py
@@ -703,11 +703,11 @@
             d1_copy(h, d).wait_send()
             d_copy(h, d).wait_send()
 
+    leads = lax.rem(lax.axis_index("head"), 2) == 0
+
     def put(u):
-        if u == 4:
-            put_stats()
-        elif u == 6:
-            put_rest()
+        if u in (4, 6):
+            pl.when(leads)((put_stats, None, put_rest)[u - 4])
         else:
             put_blocks(chain_refs[u], (q_ref, g_ref)[u % 2], u // 2)
 
@@ -731,6 +731,8 @@
     steps = plan(half)
     ahead = [("z", *c, d, 0) for c in CHAINS if c[0] == 0 for d in range(2)]
     ahead += [("z", 5, 2, d, 0) for d in range(2)] + [("ks", 0), ("ks", 1)]
+    pl.when(jnp.logical_not(leads))(put_stats)
+    pl.when(jnp.logical_not(leads))(put_rest)
     for step in ahead:
         do[step[0]](*step[1:])
     for step in steps:

time: 106 us -> 106 us (level)
  the two profiles are of different devices: /device:TPU:2 before, /device:TPU:4 now
where the time goes in v6:
time: 106 us
  Pallas kernels  102 us (96%)
  local copies, waits for them, and re-layouts  2.51 us (2%)
  between operations  1.43 us (1%)
    pallas_call x1, Pallas kernels, fast(): pl.pallas_call(functools.partial(kernel, nz), out_shape=outs, in_specs=[p...  102 us

profile of v6, /device:TPU:4, one launch (start us, length us, event | category | flops | bytes accessed | tf_op | source)
XLA Modules:
  0.0 105.9 jit_solution(10600948430287664332)
XLA Ops:
  0.6 0.0 copy-start.8
  0.6 0.0 copy-start.6
  0.7 0.0 copy-start.5
  0.7 0.0 copy-start.2
  0.7 0.0 copy-start.4
  0.7 0.0 copy-start.1
  0.7 0.0 copy-start
  0.7 0.0 copy-start.3
  0.7 101.8 %shard_map.109 = (bf16[256,256]{1,0:T(8,128)(2,1)S(1)}, bf16[256,256]{1,0:T(8,128)(2,1)S(1)}, bf16[256,256]{1,0:T(8,128)(2,1)S(1)}, f32[8,128]{1,0:T(8,128)S(1)}) custom-call(s32[2,8]{1,0:T(2,128)} %remote_ref.1, s32[2]{0:T(128)} %count_ref.1, bf16[256,256]{1,0:T(8,128)(2,1)} %q_ref.1, bf16[256,256]{1,0:T(8,128)(2,1)} %k_ref.1, bf16[256,256]{1,0:T(8,128)(2,1)} %v_ref.1, ...), custom_call_target="tpu_custom_call" | custom-call | flops 4000000000 | bytes 4194304 | tf_op jit(solution)/shard_map/pallas_call | solution.py:783
  102.5 0.5 slice.141
  103.6 0.0 copy-done.8
  103.7 0.0 copy-done.6
  103.7 0.0 copy-done.5
  103.7 0.0 copy-done.2
  103.7 0.0 copy-done.4
  103.7 0.0 copy-done.1
  103.7 0.0 copy-done
  103.7 0.0 copy-done.3
  103.7 0.2 conditional.1
  104.0 0.7 copy.284
  104.6 0.7 copy.285
  105.3 0.7 copy.286
Async XLA Ops:
  0.6 103.0 %copy-start.8 = (s32[2]{0:T(128)S(1)}, s32[2]{0:T(128)}, u32[]{:S(2)}) copy-start(s32[2]{0:T(128)} %count_ref.1) | copy-start | bytes 28
  0.6 103.0 %copy-start.6 = (s32[2,8]{1,0:T(2,128)S(1)}, s32[2,8]{1,0:T(2,128)}, u32[]{:S(2)}) copy-start(s32[2,8]{1,0:T(2,128)} %remote_ref.1) | copy-start | bytes 196
  0.7 103.0 %copy-start.5 = (f32[2,256]{1,0:T(2,128)S(1)}, f32[2,256]{1,0:T(2,128)}, u32[]{:S(2)}) copy-start(f32[2,256]{1,0:T(2,128)} %lse_ref.1) | copy-start | bytes 6148
  0.7 103.0 %copy-start.2 = (bf16[256,256]{1,0:T(8,128)(2,1)S(1)}, bf16[256,256]{1,0:T(8,128)(2,1)}, u32[]{:S(2)}) copy-start(bf16[256,256]{1,0:T(8,128)(2,1)} %g_ref.1) | copy-start | bytes 393220
  0.7 103.0 %copy-start.4 = (bf16[256,256]{1,0:T(8,128)(2,1)S(1)}, bf16[256,256]{1,0:T(8,128)(2,1)}, u32[]{:S(2)}) copy-start(bf16[256,256]{1,0:T(8,128)(2,1)} %o_ref.1) | copy-start | bytes 393220
  0.7 103.0 %copy-start.1 = (bf16[256,256]{1,0:T(8,128)(2,1)S(1)}, bf16[256,256]{1,0:T(8,128)(2,1)}, u32[]{:S(2)}) copy-start(bf16[256,256]{1,0:T(8,128)(2,1)} %v_ref.1) | copy-start | bytes 393220
  0.7 103.0 %copy-start = (bf16[256,256]{1,0:T(8,128)(2,1)S(1)}, bf16[256,256]{1,0:T(8,128)(2,1)}, u32[]{:S(2)}) copy-start(bf16[256,256]{1,0:T(8,128)(2,1)} %k_ref.1) | copy-start | bytes 393220
  0.7 103.0 %copy-start.3 = (bf16[256,256]{1,0:T(8,128)(2,1)S(1)}, bf16[256,256]{1,0:T(8,128)(2,1)}, u32[]{:S(2)}) copy-start(bf16[256,256]{1,0:T(8,128)(2,1)} %q_ref.1) | copy-start | bytes 393220

commit v7 on v5

--- a/solution.py
+++ b/solution.py
@@ -205,7 +205,7 @@
 
 
 CUT = ()
-FINE = (0, 1)
+FINE = (0,)
 CHAINS = [(u, j) for u in range(6) for j in ((0, 1) if u in FINE else (2,))]
 
 
@@ -215,7 +215,7 @@
     return half if u < 4 or d == 0 else half - 1
 
 
-def plan(half, release=(0, 1, 0), lat=1.8, chunk=0.2, tab=3.0, bw=47.0, hop=0.3, iss=0.1):
+def plan(half, release=(0, 1, 1), lat=2.0, chunk=0.2, tab=3.0, bw=46.0, hop=0.3, iss=0.15):
     mid = half // 2
     steps = {}
 

time: 106 us -> 107 us (level)
  the two profiles are of different devices: /device:TPU:2 before, /device:TPU:24 now
where the time goes in v7:
time: 107 us; the launch traced here: 106 us
  Pallas kernels  102 us (95%)
  local copies, waits for them, and re-layouts  2.51 us (2%)
  between operations  1.43 us (1%)
    pallas_call x1, Pallas kernels, fast(): pl.pallas_call(functools.partial(kernel, nz), out_shape=outs, in_specs=[p...  102 us

profile of v7, /device:TPU:24, one launch (start us, length us, event | category | flops | bytes accessed | tf_op | source)
XLA Modules:
  0.0 106.5 jit_solution(7118439578649887429)
XLA Ops:
  0.6 0.0 copy-start.8
  0.6 0.0 copy-start.6
  0.7 0.0 copy-start.5
  0.7 0.0 copy-start.2
  0.7 0.0 copy-start.4
  0.7 0.0 copy-start.1
  0.7 0.0 copy-start
  0.7 0.0 copy-start.3
  0.7 102.3 %shard_map.109 = (bf16[256,256]{1,0:T(8,128)(2,1)S(1)}, bf16[256,256]{1,0:T(8,128)(2,1)S(1)}, bf16[256,256]{1,0:T(8,128)(2,1)S(1)}, f32[8,128]{1,0:T(8,128)S(1)}) custom-call(s32[2,8]{1,0:T(2,128)} %remote_ref.1, s32[2]{0:T(128)} %count_ref.1, bf16[256,256]{1,0:T(8,128)(2,1)} %q_ref.1, bf16[256,256]{1,0:T(8,128)(2,1)} %k_ref.1, bf16[256,256]{1,0:T(8,128)(2,1)} %v_ref.1, ...), custom_call_target="tpu_custom_call" | custom-call | flops 4000000000 | bytes 4194304 | tf_op jit(solution)/shard_map/pallas_call | solution.py:781
  103.0 0.5 slice.141
  104.2 0.0 copy-done.8
  104.2 0.0 copy-done.6
  104.2 0.0 copy-done.5
  104.2 0.0 copy-done.2
  104.2 0.0 copy-done.4
  104.3 0.0 copy-done.1
  104.3 0.0 copy-done
  104.3 0.0 copy-done.3
  104.3 0.2 conditional.1
  104.5 0.7 copy.284
  105.2 0.7 copy.285
  105.8 0.7 copy.286
Async XLA Ops:
  0.6 103.6 %copy-start.8 = (s32[2]{0:T(128)S(1)}, s32[2]{0:T(128)}, u32[]{:S(2)}) copy-start(s32[2]{0:T(128)} %count_ref.1) | copy-start | bytes 28
  0.6 103.6 %copy-start.6 = (s32[2,8]{1,0:T(2,128)S(1)}, s32[2,8]{1,0:T(2,128)}, u32[]{:S(2)}) copy-start(s32[2,8]{1,0:T(2,128)} %remote_ref.1) | copy-start | bytes 196
  0.7 103.6 %copy-start.5 = (f32[2,256]{1,0:T(2,128)S(1)}, f32[2,256]{1,0:T(2,128)}, u32[]{:S(2)}) copy-start(f32[2,256]{1,0:T(2,128)} %lse_ref.1) | copy-start | bytes 6148
  0.7 103.6 %copy-start.2 = (bf16[256,256]{1,0:T(8,128)(2,1)S(1)}, bf16[256,256]{1,0:T(8,128)(2,1)}, u32[]{:S(2)}) copy-start(bf16[256,256]{1,0:T(8,128)(2,1)} %g_ref.1) | copy-start | bytes 393220
  0.7 103.6 %copy-start.4 = (bf16[256,256]{1,0:T(8,128)(2,1)S(1)}, bf16[256,256]{1,0:T(8,128)(2,1)}, u32[]{:S(2)}) copy-start(bf16[256,256]{1,0:T(8,128)(2,1)} %o_ref.1) | copy-start | bytes 393220
  0.7 103.6 %copy-start.1 = (bf16[256,256]{1,0:T(8,128)(2,1)S(1)}, bf16[256,256]{1,0:T(8,128)(2,1)}, u32[]{:S(2)}) copy-start(bf16[256,256]{1,0:T(8,128)(2,1)} %v_ref.1) | copy-start | bytes 393220
  0.7 103.6 %copy-start = (bf16[256,256]{1,0:T(8,128)(2,1)S(1)}, bf16[256,256]{1,0:T(8,128)(2,1)}, u32[]{:S(2)}) copy-start(bf16[256,256]{1,0:T(8,128)(2,1)} %k_ref.1) | copy-start | bytes 393220
  0.7 103.6 %copy-start.3 = (bf16[256,256]{1,0:T(8,128)(2,1)S(1)}, bf16[256,256]{1,0:T(8,128)(2,1)}, u32[]{:S(2)}) copy-start(bf16[256,256]{1,0:T(8,128)(2,1)} %q_ref.1) | copy-start | bytes 393220
